TPU v7x, 32 devices: a whole 2x2x4 slice. The times are simulated.
32 devices in a mesh: leaf: 4 (over y, x), row: 8 (over z, core).
Axes of the slice: x: 2, y: 2, z: 4, core: 2. Of those that a mesh axis runs over, the one named last changes fastest.
Arguments:
- sigma_root: float32 [2048, 2048], P(None, 'row')
- linv_one: bfloat16 [4, 2048, 2048], P('leaf', None, 'row'), as said below
- panel_one: bfloat16 [4, 512, 2048], P('leaf', None, 'row'), may hold values from -1.25 to 1.25
- tiles_one: int32 [4, 4], replicated, may hold values from 0 to 15, as said below
- mask_one: int32 [4, 4, 16], P('leaf', None, 'row'), may hold values 0 or 1
- linv_two: bfloat16 [4, 2048, 2048], P('leaf', None, 'row'), as said below
- panel_two: bfloat16 [4, 512, 2048], P('leaf', None, 'row'), may hold values from -1.25 to 1.25
- tiles_two: int32 [4, 4], replicated, may hold values from 0 to 15, as said below
- mask_two: int32 [4, 4, 16], P('leaf', None, 'row'), may hold values 0 or 1
- parent: int32 [4], replicated, may hold values from 0 to 3
Outputs:
- sigma_one: float32 [4, 2048, 2048], P('leaf', None, 'row')
- cross_one: float32 [4, 512, 2048], P('leaf', None, 'row')
- sigma_two: float32 [4, 2048, 2048], P('leaf', None, 'row')
- cross_two: float32 [4, 512, 2048], P('leaf', None, 'row')
Inputs may be any that keep to these rules, and one draw needn't show every extreme that they name: `tiles_one`: each row holds 4 different tile numbers in increasing order. `tiles_two`: each row holds 4 different tile numbers in increasing order. `linv_one`: each block is lower triangular with a positive diagonal. `sigma_root`: symmetric. `linv_two`: each block is lower triangular with a positive diagonal.
All inputs are finite; a program needn't handle non-finite values. No bound on the sum of `mask_one` or of `mask_two` on one device may be relied on, other than what follows from the above.
Results may differ from a plain program's by a relative error of at most 0.00045.
Values may be sent and summed in bfloat16 or wider, within the bound.
A program may use at most 64 MiB of HBM per device.

v0:
```python
import jax
import jax.numpy as jnp
from jax import lax
from jax.sharding import PartitionSpec as P

TILE = 128


def pattern_rows(tile_list):
    offsets = jnp.arange(TILE, dtype=jnp.int32)
    return (tile_list[..., None] * TILE + offsets).reshape(tile_list.shape[:-1] + (-1,))


def expand_mask(tile_mask):
    return jnp.repeat(jnp.repeat(tile_mask, TILE, axis=0), TILE, axis=1)


def assemble(selected, row_list):
    gathered = lax.all_gather(selected, "row", axis=1, tiled=True)
    return jnp.take(gathered, row_list, axis=1)


def solve_block(selected, row_list, linv_local, panel_local, mask_local):
    select = assemble(selected, row_list)
    masked = panel_local * expand_mask(mask_local).astype(jnp.bfloat16)
    linv_wide = linv_local.astype(jnp.float32)
    whole_panel = lax.all_gather(masked, "row", axis=1, tiled=True)
    upper_part = jnp.dot(whole_panel, linv_local, preferred_element_type=jnp.float32)
    cross = -jnp.dot(select, upper_part, precision=lax.Precision.HIGHEST)
    middle = linv_wide - jnp.dot(
        whole_panel.astype(jnp.float32).T, cross, precision=lax.Precision.HIGHEST
    )
    sigma = jnp.dot(
        lax.all_gather(linv_local, "row", axis=1, tiled=True).astype(jnp.float32).T,
        middle,
        precision=lax.Precision.HIGHEST,
    )
    return (sigma, cross)


def body(
    sigma_root,
    linv_one,
    panel_one,
    tiles_one,
    mask_one,
    linv_two,
    panel_two,
    tiles_two,
    mask_two,
    parent,
):
    leaf_id = lax.axis_index("leaf")
    width = sigma_root.shape[1]
    own_tiles = lax.dynamic_index_in_dim(tiles_one, leaf_id, 0, keepdims=False)
    rows_first = pattern_rows(own_tiles)
    selected_first = jnp.take(sigma_root, rows_first, axis=0)
    sigma_first, cross_first = solve_block(
        selected_first, rows_first, linv_one[0], panel_one[0], mask_one[0]
    )
    rows_every = pattern_rows(tiles_two)
    count = rows_every.shape[0]
    block_rows = rows_every.shape[1]
    owned = (parent == leaf_id).astype(jnp.float32)
    slots = jnp.take(sigma_first, rows_every.reshape(-1), axis=0).reshape(count, block_rows, width)
    slots = slots * owned[:, None, None]
    arrived = lax.all_to_all(slots, "leaf", split_axis=0, concat_axis=0, tiled=True)
    selected_second = jnp.sum(arrived, axis=0)
    rows_second = lax.dynamic_index_in_dim(rows_every, leaf_id, 0, keepdims=False)
    sigma_second, cross_second = solve_block(
        selected_second, rows_second, linv_two[0], panel_two[0], mask_two[0]
    )
    return (sigma_first[None], cross_first[None], sigma_second[None], cross_second[None])


def solution(mesh):
    return jax.shard_map(
        body,
        mesh=mesh,
        in_specs=(
            P(None, "row"),
            P("leaf", None, "row"),
            P("leaf", None, "row"),
            P(),
            P("leaf", None, "row"),
            P("leaf", None, "row"),
            P("leaf", None, "row"),
            P(),
            P("leaf", None, "row"),
            P(),
        ),
        out_specs=(
            P("leaf", None, "row"),
            P("leaf", None, "row"),
            P("leaf", None, "row"),
            P("leaf", None, "row"),
        ),
        check_vma=False,
    )
```

profile of v0, /device:TPU:0, one launch (start us, length us, event | category | flops | bytes accessed | tf_op | source)
XLA Modules:
  0.0 383.1 jit_solution(16336230606337480185)
XLA Ops:
  7.2 0.8 convert_bitcast_fusion.1
  8.8 1.7 bitcast_multiply_fusion.1
  10.6 0.7 multiply_bitcast_fusion
  11.4 2.2 gather_fusion
  13.7 2.1 broadcast_select_fusion
  17.3 0.7 bitcast_multiply_fusion
  18.4 25.8 %all-gather.9.cloned.1.call-done = bf16[512,2048]{1,0:T(8,128)(2,1)} async-done(((bf16[512,256]{1,0:T(8,128)(2,1)}), bf16[512,2048]{1,0:T(8,128)(2,1)}) %all-gather.9.cloned.1.call-update) | async-done | bytes 2097168 | tf_op jit(solution)/shard_map/all_gather | solution.py:27
  44.2 3.1 fusion.11
  47.3 45.3 %all-gather.11.cloned.1.call-done = f32[512,2048]{1,0:T(8,128)} async-done(((f32[512,256]{1,0:T(8,128)}), f32[512,2048]{1,0:T(8,128)}) %all-gather.11.cloned.1.call-update) | async-done | bytes 4194320 | tf_op jit(solution)/shard_map/all_gather | solution.py:19
  92.6 5.3 %copy.21 = f32[512,2048]{0,1:T(8,128)} copy(f32[512,2048]{1,0:T(8,128)} %all-gather.11.cloned.1.call-done) | data formatting | bytes 8388608 | tf_op jit(solution)/shard_map/all_gather | solution.py:19
  98.0 4.5 %gather_fusion.2 = f32[512,512]{1,0:T(8,128)S(1)} fusion(f32[512,2048]{0,1:T(8,128)} %copy.21, s32[1024]{0:T(1024)S(1)} %pad_clamp_fusion.1), kind=kCustom, calls=%fused_computation.clone | custom fusion | bytes 2099200 | tf_op jit(solution)/shard_map/jit(_take)/gather | solution.py:20
  102.5 3.0 convolution_negate_fusion.1
  105.5 0.8 copy-done.5
  106.3 5.5 %convolution_subtract_fusion.1 = f32[2048,256]{1,0:T(8,128)} fusion(bf16[512,2048]{1,0:T(8,128)(2,1)} %all-gather.9.cloned.1.call-done, f32[512,256]{1,0:T(8,128)S(1)} %convolution_negate_fusion.1, bf16[1,2048,256]{2,1,0:T(8,128)(2,1)S(1)} %copy-done.2), kind=kOutput, calls=%fused_computation.10 | convolution fusion | flops 3222274048 | bytes 5767168 | tf_op jit(solution)/shard_map/dot_general | solution.py:30
  111.8 63.7 %all-gather.17.cloned.1.call-done = bf16[1,2048,2048]{2,1,0:T(8,128)(2,1)} async-done(((bf16[1,2048,256]{2,1,0:T(8,128)(2,1)}), bf16[1,2048,2048]{2,1,0:T(8,128)(2,1)}) %all-gather.17.cloned.1.call-update) | async-done | bytes 8388624 | tf_op jit(solution)/shard_map/all_gather | solution.py:34
  175.5 10.8 %fusion.2 = f32[256,2048]{1,0:T(8,128)} fusion(f32[2048,256]{1,0:T(8,128)} %convolution_subtract_fusion.1, bf16[1,2048,2048]{2,1,0:T(8,128)(2,1)} %all-gather.17.cloned.1.call-done), kind=kOutput, calls=%fused_computation.6 | convolution fusion | flops 12884901888 | bytes 12582912 | tf_op jit(solution)/shard_map/dot_general | solution.py:33
  186.3 2.9 copy.23
  189.1 10.2 %gather_fusion.1 = f32[2048,256]{1,0:T(8,128)} fusion(f32[2048,256]{1,0:T(8,128)} %copy.23, s32[2048]{0:T(1024)S(1)} %broadcast_clamp_fusion), kind=kCustom, calls=%fused_computation.3 | custom fusion | bytes 4202496 | tf_op jit(solution)/shard_map/jit(_take)/gather | solution.py:65
  199.4 1.8 select_multiply_fusion
  201.2 29.4 %all_to_all.5 = f32[4,512,256]{2,1,0:T(8,128)} all-to-all(f32[4,512,256]{2,1,0:T(8,128)S(1)} %select_multiply_fusion), channel_id=1, replica_groups=mesh['leaf'=4,'row'=8] {'leaf'}, dimensions={0} | all-to-all | bytes 4194304 | tf_op jit(solution)/shard_map/all_to_all | solution.py:67
  230.5 2.7 reduce_sum.9
  233.2 2.0 copy.24
  235.9 3.1 fusion.8
  239.0 3.0 copy.25
  242.0 37.8 %all-gather.15.cloned.1.call-done = f32[512,2048]{0,1:T(8,128)} async-done(((f32[512,256]{0,1:T(8,128)}), f32[512,2048]{0,1:T(8,128)}) %all-gather.15.cloned.1.call-update) | async-done | bytes 4194320 | tf_op jit(solution)/shard_map/all_gather | solution.py:19
  279.9 4.2 %gather_fusion.3 = f32[512,512]{1,0:T(8,128)S(1)} fusion(f32[512,2048]{0,1:T(8,128)} %all-gather.15.cloned.1.call-done, s32[1024]{0:T(1024)S(1)} %pad_clamp_fusion), kind=kCustom, calls=%fused_computation.1.clone | custom fusion | bytes 2099200 | tf_op jit(solution)/shard_map/jit(_take)/gather | solution.py:20
  284.1 3.0 convolution_negate_fusion
  287.1 0.8 copy-done.6
  287.9 5.6 %convolution_subtract_fusion = f32[2048,256]{1,0:T(8,128)} fusion(bf16[512,2048]{1,0:T(8,128)(2,1)} %all-gather.13.cloned.1.call-done, f32[512,256]{1,0:T(8,128)S(1)} %convolution_negate_fusion, bf16[1,2048,256]{2,1,0:T(8,128)(2,1)S(1)} %copy-done.4), kind=kOutput, calls=%fused_computation.9 | convolution fusion | flops 3222274048 | bytes 5767168 | tf_op jit(solution)/shard_map/dot_general | solution.py:30
  293.6 69.0 %all-gather.19.cloned.1.call-done = bf16[1,2048,2048]{2,1,0:T(8,128)(2,1)} async-done(((bf16[1,2048,256]{2,1,0:T(8,128)(2,1)}), bf16[1,2048,2048]{2,1,0:T(8,128)(2,1)}) %all-gather.19.cloned.1.call-update) | async-done | bytes 8388624 | tf_op jit(solution)/shard_map/all_gather | solution.py:34
  362.6 10.8 %fusion.4 = f32[1,2048,256]{1,2,0:T(8,128)} fusion(f32[2048,256]{1,0:T(8,128)} %convolution_subtract_fusion, bf16[1,2048,2048]{2,1,0:T(8,128)(2,1)} %all-gather.19.cloned.1.call-done), kind=kOutput, calls=%fused_computation.8 | convolution fusion | flops 12884901888 | bytes 12582912 | tf_op jit(solution)/shard_map/dot_general | solution.py:33
  373.4 2.9 copy.26
  (59 shorter events, 3.5 us)
Async XLA Ops:
  7.2 4.2 %copy-start = (f32[2048,256]{1,0:T(8,128)S(1)}, f32[2048,256]{1,0:T(8,128)}, u32[]{:S(2)}) copy-start(f32[2048,256]{1,0:T(8,128)} %param.12) | copy-start | bytes 6291460
  7.2 37.0 %all-gather.9.cloned.1.call-start = ((), (), s32[]{:S(2)}) async-start(), calls=%async_computation.1 | async-start | bytes 2359296 | tf_op jit(solution)/shard_map/all_gather | solution.py:27
  10.5 82.1 %all-gather.11.cloned.1.call-start = ((), (), s32[]{:S(2)}) async-start(), calls=%async_computation.2 | async-start | bytes 4718592 | tf_op jit(solution)/shard_map/all_gather | solution.py:19
  13.6 3.0 copy-start.9
  13.6 3.7 copy-start.7
  13.7 4.6 %copy-start.8 = (s32[4,4]{1,0:T(4,128)S(1)}, s32[4,4]{1,0:T(4,128)}, u32[]{:S(2)}) copy-start(s32[4,4]{1,0:T(4,128)} %param.19) | copy-start | bytes 196
  13.7 4.7 %copy-start.10 = (s32[4]{0:T(128)S(1)}, s32[4]{0:T(128)}, u32[]{:S(2)}) copy-start(s32[4]{0:T(128)} %param.21) | copy-start | bytes 52
  13.7 30.5 %copy-start.1 = (bf16[1,2048,256]{2,1,0:T(8,128)(2,1)S(1)}, bf16[1,2048,256]{2,1,0:T(8,128)(2,1)}, u32[]{:S(2)}) copy-start(bf16[1,2048,256]{2,1,0:T(8,128)(2,1)} %param.13) | copy-start | bytes 3145732
  15.8 159.7 %all-gather.17.cloned.1.call-start = ((), (), s32[]{:S(2)}) async-start(), calls=%async_computation.5 | async-start | bytes 9437184 | tf_op jit(solution)/shard_map/all_gather | solution.py:34
  16.5 219.4 %all-gather.13.cloned.1.call-start = ((), (), s32[]{:S(2)}) async-start(), calls=%async_computation.3 | async-start | bytes 2359296 | tf_op jit(solution)/shard_map/all_gather | solution.py:27
  18.1 261.8 %all-gather.15.cloned.1.call-start = ((), (), s32[]{:S(2)}) async-start(), calls=%async_computation.4 | async-start | bytes 4718592 | tf_op jit(solution)/shard_map/all_gather | solution.py:19
  102.5 3.9 %copy-start.2 = (bf16[1,2048,256]{2,1,0:T(8,128)(2,1)S(1)}, bf16[1,2048,256]{2,1,0:T(8,128)(2,1)}, u32[]{:S(2)}) copy-start(bf16[1,2048,256]{2,1,0:T(8,128)(2,1)} %param.13) | copy-start | bytes 3145732
  105.5 0.8 copy-start.5
  230.5 5.4 %copy-start.3 = (bf16[1,2048,256]{2,1,0:T(8,128)(2,1)S(1)}, bf16[1,2048,256]{2,1,0:T(8,128)(2,1)}, u32[]{:S(2)}) copy-start(bf16[1,2048,256]{2,1,0:T(8,128)(2,1)} %param.17) | copy-start | bytes 3145732
  235.2 127.3 %all-gather.19.cloned.1.call-start = ((), (), s32[]{:S(2)}) async-start(), calls=%async_computation.6 | async-start | bytes 9437184 | tf_op jit(solution)/shard_map/all_gather | solution.py:34
  284.1 3.8 %copy-start.4 = (bf16[1,2048,256]{2,1,0:T(8,128)(2,1)S(1)}, bf16[1,2048,256]{2,1,0:T(8,128)(2,1)}, u32[]{:S(2)}) copy-start(bf16[1,2048,256]{2,1,0:T(8,128)(2,1)} %param.17) | copy-start | bytes 3145732
  287.1 0.8 copy-start.6
Sparse Core Ops, SparseCore 0:
  10.6 33.5 all-gather.8
  46.4 46.2 all-gather.10
  94.2 81.2 all-gather.16
  176.9 29.0 all-gather.12
  235.4 44.4 all-gather.14
  281.3 81.2 all-gather.18
where the time goes:
time: 384 us; the launch traced here: 383 us
  waiting for transfers between devices  243 us (63%)
  matrix products  45 us (12%)
  local copies, waits for them, and re-layouts  40.4 us (11%)
  blocking collectives  29.4 us (8%)
  between operations  14.4 us (4%)
  other arithmetic  10.8 us (3%)
    all_gather x2, waiting for transfers between devices, solve_block(): lax.all_gather(linv_local, 'row', axis=1, tiled=True).astype(jnp.float32)  133 us
    all_gather x2, waiting for transfers between devices, assemble(): gathered = lax.all_gather(selected, 'row', axis=1, tiled=True)  83.1 us
    all_to_all x1, blocking collectives, body(): lax.all_to_all(slots, 'leaf', split_axis=0, concat_axis=0, tiled=True)  29.4 us
    all_gather x2, waiting for transfers between devices, solve_block(): whole_panel = lax.all_gather(masked, 'row', axis=1, tiled=True)  25.8 us
    dot_general x2, matrix products, solve_block(): jnp.dot(lax.all_gather(linv_local, 'row', axis=1, tiled=True).astype(jnp....  21.6 us
    dot_general x2, matrix products, solve_block(): jnp.dot(whole_panel.astype(jnp.float32).T, cross, precision=lax.Precision...  11.1 us
    gather x1, local copies, waits for them, and re-layouts, body(): jnp.take(sigma_first, rows_every.reshape(-1), axis=0)  10.2 us
    gather x2, local copies, waits for them, and re-layouts, assemble(): return jnp.take(gathered, row_list, axis=1)  8.7 us
  transfers between devices with their start and end apart: 6, of which 5 were waited for; matrix products, arithmetic and copies ran while one was open for 20% of the time, Pallas kernels for 0%

commit v1 on v0

v1 whole, which is shorter than its diff:
```python
import functools

import jax
import jax.numpy as jnp
from jax import lax
from jax.experimental import pallas as pl
from jax.experimental.pallas import tpu as pltpu
from jax.sharding import PartitionSpec as P

TILE = 128
MESH = pl.DeviceIdType.MESH
HIGH = lax.Precision.HIGH


def pattern_rows(tile_list):
    offsets = jnp.arange(TILE, dtype=jnp.int32)
    return (tile_list[..., None] * TILE + offsets).reshape(tile_list.shape[:-1] + (-1,))


def expand_mask(tile_mask):
    return jnp.repeat(jnp.repeat(tile_mask, TILE, axis=0), TILE, axis=1)


def gather_kernel(chips, panel_ref, linv_ref, whole_panel, *rest):
    blocks = rest[:chips]
    zrecv, zright, zleft, srecv, ssend, local = rest[chips:]
    width = panel_ref.shape[1]
    step = 2 * width
    row = lax.axis_index("row")
    z = lax.div(row, 2)
    core = lax.rem(row, 2)
    right, left, sibling = row + 2, row - 2, row + 1 - 2 * core

    barrier = pltpu.get_barrier_semaphore()

    def greet(device):
        pl.semaphore_signal(barrier, inc=1, device_id={"row": device}, device_id_type=MESH)

    greet(sibling)

    @pl.when(z > 0)
    def _():
        greet(left)

    @pl.when(z < chips - 1)
    def _():
        greet(right)

    @pl.when(jnp.logical_or(z == 0, z == chips - 1))
    def _():
        pl.semaphore_wait(barrier, 2)

    @pl.when(jnp.logical_and(z > 0, z < chips - 1))
    def _():
        pl.semaphore_wait(barrier, 3)

    def place(s, c, piece):
        if piece == 0:
            return whole_panel.at[:, pl.ds(pl.multiple_of((2 * s + c) * width, width), width)]
        return blocks[s].at[pl.ds((piece - 1) * step, step), pl.ds(pl.multiple_of(c * width, width), width)]

    def origin(s, piece):
        if piece == 0:
            return panel_ref
        return linv_ref.at[pl.ds((s + piece - 1) * step, step), :]

    def send(source, s, piece, sends, recvs, device):
        return pltpu.make_async_remote_copy(
            src_ref=source,
            dst_ref=place(s, core, piece),
            send_sem=sends.at[s, piece],
            recv_sem=recvs.at[s, piece],
            device_id={"row": device},
            device_id_type=MESH,
        )

    def pieces(s):
        return range(1 + chips - s)

    def copies(source, s, piece, go_right, go_left):
        out = []
        if go_right:
            out.append(send(source, s, piece, zright, zrecv, right))
        if go_left:
            out.append(send(source, s, piece, zleft, zrecv, left))
        out.append(send(source, s, piece, ssend, srecv, sibling))
        return out

    def own(s, piece):
        here = pltpu.make_async_copy(origin(s, piece), place(s, core, piece), local.at[piece])
        return copies(origin(s, piece), s, piece, s < chips - 1, s > 0) + [here]

    for s in range(chips):
        @pl.when(z == s)
        def _(s=s):
            for piece in pieces(s):
                for copy in own(s, piece):
                    copy.start()

    def routes(hops):
        for s in range(chips):
            if s + hops < chips:
                yield s, s + hops, s + hops < chips - 1, False
            if s - hops >= 0:
                yield s, s - hops, False, s - hops > 0

    def arrived(s, piece, recvs, c):
        pltpu.make_async_copy(place(s, c, piece), place(s, c, piece), recvs.at[s, piece]).wait()

    for hops in range(1, chips):
        for piece in range(chips + 1):
            for s, here, go_right, go_left in routes(hops):
                if piece in pieces(s):
                    @pl.when(z == here)
                    def _(s=s, piece=piece, go_right=go_right, go_left=go_left):
                        arrived(s, piece, zrecv, core)
                        for copy in copies(place(s, core, piece), s, piece, go_right, go_left):
                            copy.start()

    for s in range(chips):
        for piece in pieces(s):
            arrived(s, piece, srecv, 1 - core)

        @pl.when(z == s)
        def _(s=s):
            for piece in pieces(s):
                moves = own(s, piece)
                for copy in moves[:-1]:
                    copy.wait_send()
                moves[-1].wait()

    for hops in range(1, chips):
        for s, here, go_right, go_left in routes(hops):
            @pl.when(z == here)
            def _(s=s, go_right=go_right, go_left=go_left):
                for piece in pieces(s):
                    for copy in copies(place(s, core, piece), s, piece, go_right, go_left):
                        copy.wait_send()


def gather_block(panel, linv, chips, number):
    order, width = linv.shape
    rows = panel.shape[0]
    step = 2 * width
    kind = linv.dtype
    any_space = pl.BlockSpec(memory_space=pl.ANY)
    shapes = [jax.ShapeDtypeStruct((rows, order), kind)]
    shapes += [jax.ShapeDtypeStruct((order - s * step, step), kind) for s in range(chips)]
    moved = (rows * order + order * order) * 2
    out = pl.pallas_call(
        functools.partial(gather_kernel, chips),
        out_shape=shapes,
        in_specs=[any_space, any_space],
        out_specs=[any_space] * len(shapes),
        scratch_shapes=[pltpu.SemaphoreType.DMA((chips, chips + 1))] * 5
        + [pltpu.SemaphoreType.DMA((chips + 1,))],
        compiler_params=pltpu.CompilerParams(collective_id=number, has_side_effects=True),
        cost_estimate=pl.CostEstimate(flops=0, bytes_accessed=moved * 20, transcendentals=0),
        name="gather_%d" % number,
    )(panel, linv)
    return out[0], out[1:]


def spread_tiles(selected, tile_list):
    width = selected.shape[1]
    per = width // TILE
    row = lax.axis_index("row")
    parts = []
    for a in range(tile_list.shape[0]):
        tile = tile_list[a]
        piece = jnp.zeros((selected.shape[0], TILE), selected.dtype)
        for k in range(per):
            hit = tile == row * per + k
            piece = piece + jnp.where(hit, selected[:, k * TILE:(k + 1) * TILE], 0.0)
        parts.append(piece)
    return jnp.concatenate(parts, axis=1)


def finish_block(select, whole_panel, blocks, linv):
    width = linv.shape[1]
    step = 2 * width
    row = lax.axis_index("row")
    upper = jnp.concatenate(
        [
            jnp.dot(whole_panel[:, s * step:], block, preferred_element_type=jnp.float32)
            for s, block in enumerate(blocks)
        ],
        axis=1,
    )
    own = lax.dynamic_slice_in_dim(upper, row * width, width, 1)
    cross = -jnp.dot(select, own, precision=HIGH)
    gram = jnp.concatenate(
        [
            lax.dot_general(
                block, linv[s * step:], (((0,), (0,)), ((), ())), preferred_element_type=jnp.float32
            )
            for s, block in enumerate(blocks)
        ],
        axis=0,
    )
    sigma = gram - lax.dot_general(upper, cross, (((0,), (0,)), ((), ())), precision=HIGH)
    return sigma, cross


def body(
    chips,
    sigma_root,
    linv_one,
    panel_one,
    tiles_one,
    mask_one,
    linv_two,
    panel_two,
    tiles_two,
    mask_two,
    parent,
):
    leaf_id = lax.axis_index("leaf")
    width = sigma_root.shape[1]
    own_tiles = lax.dynamic_index_in_dim(tiles_one, leaf_id, 0, keepdims=False)
    selected_first = jnp.take(sigma_root, pattern_rows(own_tiles), axis=0)
    select_first = lax.psum(spread_tiles(selected_first, own_tiles), "row")
    masked_one = panel_one[0] * expand_mask(mask_one[0]).astype(jnp.bfloat16)
    masked_two = panel_two[0] * expand_mask(mask_two[0]).astype(jnp.bfloat16)
    whole_one, blocks_one = gather_block(masked_one, linv_one[0], chips, 0)
    sigma_first, cross_first = finish_block(select_first, whole_one, blocks_one, linv_one[0])
    rows_every = pattern_rows(tiles_two)
    count, block_rows = rows_every.shape
    owned = (parent == leaf_id).astype(jnp.float32)
    slots = jnp.take(sigma_first, rows_every.reshape(-1), axis=0).reshape(count, block_rows, width)
    slots = slots * owned[:, None, None]
    arrived = lax.all_to_all(slots, "leaf", split_axis=0, concat_axis=0, tiled=True)
    arrived, masked_two, linv_second = lax.optimization_barrier((arrived, masked_two, linv_two[0]))
    selected_second = jnp.sum(arrived, axis=0)
    tiles_second = lax.dynamic_index_in_dim(tiles_two, leaf_id, 0, keepdims=False)
    select_second = lax.psum(spread_tiles(selected_second, tiles_second), "row")
    whole_two, blocks_two = gather_block(masked_two, linv_second, chips, 1)
    sigma_second, cross_second = finish_block(select_second, whole_two, blocks_two, linv_second)
    return (sigma_first[None], cross_first[None], sigma_second[None], cross_second[None])


def solution(mesh):
    chips = mesh.shape["row"] // 2
    return jax.shard_map(
        functools.partial(body, chips),
        mesh=mesh,
        in_specs=(
            P(None, "row"),
            P("leaf", None, "row"),
            P("leaf", None, "row"),
            P(),
            P("leaf", None, "row"),
            P("leaf", None, "row"),
            P("leaf", None, "row"),
            P(),
            P("leaf", None, "row"),
            P(),
        ),
        out_specs=(
            P("leaf", None, "row"),
            P("leaf", None, "row"),
            P("leaf", None, "row"),
            P("leaf", None, "row"),
        ),
        check_vma=False,
    )
```

time: 384 us -> 351 us (0.914)
  waiting for transfers between devices: 243 us -> 91.1 us
  Pallas kernels: 0 us -> 146 us
  blocking collectives: 29.4 us -> 0 us
  local copies, waits for them, and re-layouts: 40.4 us -> 15.8 us
  between operations: 14.4 us -> 24.9 us
  other arithmetic: 10.8 us -> 19.6 us
  starting transfers between devices: 0.42 us -> 4.65 us
    all_gather x6 -> x0, waiting for transfers between devices: 242 us -> none  [the longest x2 133 us: solve_block(): lax.all_gather(linv_local, 'row', axis=1, tiled=True).astype(jnp.float32)]
    pallas_call x0 -> x2, Pallas kernels: none -> 146 us  [gather_block(): pl.pallas_call(functools.partial(gather_kernel, chips), out_shape=shapes,...]
    psum x0 -> x2, waiting for transfers between devices: none -> 72.9 us  [the longest x1 72.9 us: body(): select_second = lax.psum(spread_tiles(selected_second, tiles_second), 'row')]
    all_to_all x1 -> x0, blocking collectives: 29.4 us -> none  [body(): lax.all_to_all(slots, 'leaf', split_axis=0, concat_axis=0, tiled=True)]
    all_to_all x0 -> x1, waiting for transfers between devices: none -> 18.2 us  [body(): lax.all_to_all(slots, 'leaf', split_axis=0, concat_axis=0, tiled=True)]
    concatenate x0 -> x4, other arithmetic: none -> 10.3 us  [the longest x2 8.21 us: finish_block(): jnp.concatenate([jnp.dot(whole_panel[:, s * step:], block, preferred_elem...]
    gather x3 -> x1, local copies, waits for them, and re-layouts: 10.9 us -> 1.57 us  [body(): selected_first = jnp.take(sigma_root, pattern_rows(own_tiles), axis=0)]
    unnamed x26 -> x56, local copies, waits for them, and re-layouts: 7.5 us -> 1.27 us
  transfers between devices with their start and end apart: 6 -> 3, of which waited for: 5 -> 2; matrix products, arithmetic and copies ran while one was open for 20% -> 9% of each run, Pallas kernels for 0% -> 22%
where the time goes in v1:
time: 351 us; the launch traced here: 350 us
  Pallas kernels  146 us (42%)
  waiting for transfers between devices  91.1 us (26%)
  matrix products  48.2 us (14%)
  between operations  24.9 us (7%)
  other arithmetic  19.6 us (6%)
  local copies, waits for them, and re-layouts  15.8 us (5%)
  starting transfers between devices  4.65 us (1%)
    pallas_call x2, Pallas kernels, gather_block(): pl.pallas_call(functools.partial(gather_kernel, chips), out_shape=shapes,...  146 us
    psum x1, waiting for transfers between devices, body(): select_second = lax.psum(spread_tiles(selected_second, tiles_second), 'row')  72.9 us
    dot_general x8, matrix products, finish_block(): jnp.dot(whole_panel[:, s * step:], block, preferred_element_type=jnp.floa...  19 us
    all_to_all x1, waiting for transfers between devices, body(): lax.all_to_all(slots, 'leaf', split_axis=0, concat_axis=0, tiled=True)  18.2 us
    dot_general x8, matrix products, finish_block(): lax.dot_general(block, linv[s * step:], (((0,), (0,)), ((), ())), preferr...  14.2 us
    dot_general x2, matrix products, finish_block(): lax.dot_general(upper, cross, (((0,), (0,)), ((), ())), precision=HIGH)  10.8 us
    gather x1, local copies, waits for them, and re-layouts, body(): jnp.take(sigma_first, rows_every.reshape(-1), axis=0)  10.2 us
    concatenate x2, other arithmetic, finish_block(): jnp.concatenate([jnp.dot(whole_panel[:, s * step:], block, preferred_elem...  8.21 us
  transfers between devices with their start and end apart: 3, of which 2 were waited for; matrix products, arithmetic and copies ran while one was open for 9% of the time, Pallas kernels for 22%

profile of v1, /device:TPU:0, one launch (start us, length us, event | category | flops | bytes accessed | tf_op | source)
XLA Modules:
  0.0 350.2 jit_solution(5164955638640142623)
XLA Ops:
  14.0 1.6 gather_fusion
  18.5 78.0 %gather_0.1 = (bf16[512,2048]{1,0:T(8,128)(2,1)}, bf16[2048,512]{1,0:T(8,128)(2,1)}, bf16[1536,512]{1,0:T(8,128)(2,1)}, bf16[1024,512]{1,0:T(8,128)(2,1)}, bf16[512,512]{1,0:T(8,128)(2,1)}) custom-call(bf16[512,256]{1,0:T(8,128)(2,1)} %bitcast_multiply_fusion.1.panel_ref, bf16[2048,256]{1,0:T(8,128)(2,1)} %bitcast.84), custom_call_target="tpu_custom_call" | custom-call | bytes 209715200 | tf_op jit(solution)/shard_map/gather_0/pallas_call | solution.py:150
  96.5 3.3 fusion.33
  99.8 4.0 %fusion.37 = f32[512,512]{0,1:T(8,128)} fusion(bf16[512,2048]{1,0:T(8,128)(2,1)} %get-tuple-element.21, bf16[2048,512]{1,0:T(8,128)(2,1)S(1)} %copy-done.6), kind=kOutput, calls=%fused_computation.76 | convolution fusion | flops 1073741824 | bytes 5242880 | tf_op jit(solution)/shard_map/dot_general | solution.py:185
  103.8 1.4 fusion.9
  105.4 2.1 fusion.3
  107.5 1.3 fusion.14
  108.8 1.8 fusion.7
  110.6 1.5 fusion.22
  112.1 1.1 fusion.25
  113.3 4.6 %pad_maximum_fusion = f32[512,2048]{0,1:T(8,128)} fusion(f32[512,512]{0,1:T(8,128)} %fusion.22, f32[512,512]{0,1:T(8,128)} %fusion.7, f32[512,512]{0,1:T(8,128)} %fusion.3, f32[512,512]{0,1:T(8,128)} %fusion.37), kind=kLoop, calls=%fused_computation.2 | loop fusion | flops 3145728 | bytes 8388608 | tf_op jit(solution)/shard_map/concatenate | solution.py:183
  117.9 2.1 convolution_negate_fusion.1
  120.9 5.3 %convolution_subtract_fusion.1 = f32[2048,256]{1,0:T(8,128)} fusion(f32[512,256]{1,0:T(8,128)S(1)} %convolution_negate_fusion.1, f32[512,256]{1,0:T(8,128)} %fusion.25, f32[512,256]{1,0:T(8,128)} %fusion.14, f32[512,256]{1,0:T(8,128)} %fusion.9, f32[512,256]{1,0:T(8,128)} %fusion.33, f32[512,512]{0,1:T(8,128)S(1)} %copy-done.3, f32[512,512]{0,1:T(8,128)} %fusion.7, ...), kind=kOutput, calls=%fused_computation.6 | convolution fusion | flops 1615855616 | bytes 8912896 | tf_op jit(solution)/shard_map/dot_general | solution.py:201
  126.2 10.2 %gather_fusion.1 = f32[2048,256]{1,0:T(8,128)} fusion(f32[2048,256]{1,0:T(8,128)} %convolution_subtract_fusion.1, s32[2048]{0:T(1024)S(1)} %broadcast_clamp_fusion), kind=kCustom, calls=%fused_computation.1 | custom fusion | bytes 4202496 | tf_op jit(solution)/shard_map/jit(_take)/gather | solution.py:230
  136.4 2.8 select_multiply_fusion
  139.1 4.6 %all-to-all-start = ((f32[4,512,256]{2,1,0:T(8,128)}), f32[4,512,256]{2,1,0:T(8,128)}, u32[]{:S(2)}, u32[]{:S(2)}) async-start(f32[4,512,256]{2,1,0:T(8,128)} %select_multiply_fusion), calls=%async_computation | async-start | bytes 4194304 | tf_op jit(solution)/shard_map/all_to_all | solution.py:232
  151.3 18.2 %all-to-all-done = f32[4,512,256]{2,1,0:T(8,128)} async-done(((f32[4,512,256]{2,1,0:T(8,128)}), f32[4,512,256]{2,1,0:T(8,128)}, u32[]{:S(2)}, u32[]{:S(2)}) %all-to-all-start) | async-done | bytes 2097184 | tf_op jit(solution)/shard_map/all_to_all | solution.py:232
  169.5 67.9 %gather_1.1 = (bf16[512,2048]{1,0:T(8,128)(2,1)}, bf16[2048,512]{1,0:T(8,128)(2,1)}, bf16[1536,512]{1,0:T(8,128)(2,1)}, bf16[1024,512]{1,0:T(8,128)(2,1)}, bf16[512,512]{1,0:T(8,128)(2,1)}) custom-call(bf16[512,256]{1,0:T(8,128)(2,1)} %bitcast_multiply_fusion.panel_ref, bf16[2048,256]{1,0:T(8,128)(2,1)} %bitcast.85), custom_call_target="tpu_custom_call" | custom-call | bytes 209715200 | tf_op jit(solution)/shard_map/gather_1/pallas_call | solution.py:150
  237.4 3.3 fusion.38
  240.7 4.0 %fusion.39 = f32[512,512]{0,1:T(8,128)} fusion(bf16[512,2048]{1,0:T(8,128)(2,1)} %get-tuple-element.28, bf16[2048,512]{1,0:T(8,128)(2,1)S(1)} %copy-done.7), kind=kOutput, calls=%fused_computation.78 | convolution fusion | flops 1073741824 | bytes 5242880 | tf_op jit(solution)/shard_map/dot_general | solution.py:185
  244.7 1.4 fusion.11
  246.3 2.1 fusion.1
  248.4 1.3 fusion.19
  249.7 1.7 fusion.5
  251.4 2.6 reduce_sum.9
  254.0 1.1 select_add_fusion.3
  256.2 1.8 fusion.17
  258.1 1.1 fusion.27
  259.2 3.6 %pad_maximum_fusion.1 = f32[512,2048]{0,1:T(8,128)} fusion(f32[512,512]{0,1:T(8,128)S(1)} %fusion.17, f32[512,512]{0,1:T(8,128)} %fusion.5, f32[512,512]{0,1:T(8,128)S(1)} %copy-done.12, f32[512,512]{0,1:T(8,128)S(1)} %copy-done.10), kind=kLoop, calls=%fused_computation.3 | loop fusion | flops 3145728 | bytes 8388608 | tf_op jit(solution)/shard_map/concatenate | solution.py:183
  262.8 72.9 %all-reduce.5.cloned.1.call-done = f32[512,512]{1,0:T(8,128)} async-done(((f32[512,512]{1,0:T(8,128)}), f32[512,512]{1,0:T(8,128)}) %all-reduce.5.cloned.1.call-update) | async-done | bytes 1048592 | tf_op jit(solution)/shard_map/psum | solution.py:236
  335.8 2.1 convolution_negate_fusion
  337.9 5.5 %fusion = f32[1,2048,256]{2,1,0:T(8,128)} fusion(f32[512,256]{1,0:T(8,128)S(1)} %convolution_negate_fusion, f32[512,256]{1,0:T(8,128)} %fusion.27, f32[512,256]{1,0:T(8,128)} %fusion.19, f32[512,256]{1,0:T(8,128)} %fusion.11, f32[512,256]{1,0:T(8,128)} %fusion.38, f32[512,512]{0,1:T(8,128)S(1)} %copy-done.5, f32[512,512]{0,1:T(8,128)} %fusion.5, ...), kind=kOutput, calls=%fused_computation.5 | convolution fusion | flops 1615855616 | bytes 8912896 | tf_op jit(solution)/shard_map/dot_general | solution.py:201
  (89 shorter events, 9.0 us)
Async XLA Ops:
  7.2 6.9 %copy-start = (f32[2048,256]{1,0:T(8,128)S(1)}, f32[2048,256]{1,0:T(8,128)}, u32[]{:S(2)}) copy-start(f32[2048,256]{1,0:T(8,128)} %param.10) | copy-start | bytes 6291460
  7.2 110.7 %all-reduce.3.cloned.1.call-start = ((), (), s32[]{:S(2)}) async-start(), calls=%async_computation.1 | async-start | bytes 2097152 | tf_op jit(solution)/shard_map/psum | solution.py:222
  15.7 1.2 copy-start.25
  15.9 1.8 copy-start.16
  16.9 79.6 %copy-start.1 = (bf16[1,2048,256]{2,1,0:T(8,128)(2,1)S(1)}, bf16[1,2048,256]{2,1,0:T(8,128)(2,1)}, u32[]{:S(2)}) copy-start(bf16[1,2048,256]{2,1,0:T(8,128)(2,1)} %param.11) | copy-start | bytes 3145732
  96.5 3.3 copy-start.6
  99.8 4.0 %copy-start.21 = (bf16[1536,512]{1,0:T(8,128)(2,1)S(1)}, bf16[1536,512]{1,0:T(8,128)(2,1)}, u32[]{:S(2)}) copy-start(bf16[1536,512]{1,0:T(8,128)(2,1)} %get-tuple-element.18) | copy-start | bytes 4718596
  103.8 1.6 copy-start.19
  105.4 2.1 copy-start.23
  108.8 1.8 copy-start.9
  110.6 2.6 copy-start.20
  110.6 2.7 copy-start.27
  117.9 2.9 copy-start.3
  117.9 2.9 copy-start.13
  120.1 0.8 copy-start.14
  139.1 10.7 %copy-start.26 = (s32[1,4,2]{1,2,0:T(2,128)S(1)}, s32[1,4,2]{1,2,0:T(2,128)}, u32[]{:S(2)}) copy-start(s32[1,4,2]{1,2,0:T(2,128)} %param.18) | copy-start | bytes 100
  139.1 11.4 %copy-start.17 = (bf16[1,512,256]{2,1,0:T(8,128)(2,1)S(1)}, bf16[1,512,256]{2,1,0:T(8,128)(2,1)}, u32[]{:S(2)}) copy-start(bf16[1,512,256]{2,1,0:T(8,128)(2,1)} %param.16) | copy-start | bytes 786436
  139.1 30.3 %all-to-all-start = ((f32[4,512,256]{2,1,0:T(8,128)}), f32[4,512,256]{2,1,0:T(8,128)}, u32[]{:S(2)}, u32[]{:S(2)}) async-start(f32[4,512,256]{2,1,0:T(8,128)} %select_multiply_fusion), calls=%async_computation | async-start | bytes 4194304 | tf_op jit(solution)/shard_map/all_to_all | solution.py:232
  143.7 93.7 %copy-start.2 = (bf16[1,2048,256]{2,1,0:T(8,128)(2,1)S(1)}, bf16[1,2048,256]{2,1,0:T(8,128)(2,1)}, u32[]{:S(2)}) copy-start(bf16[1,2048,256]{2,1,0:T(8,128)(2,1)} %param.15) | copy-start | bytes 3145732
  143.7 192.0 %all-reduce.5.cloned.1.call-start = ((), (), s32[]{:S(2)}) async-start(), calls=%async_computation.2 | async-start | bytes 2097152 | tf_op jit(solution)/shard_map/psum | solution.py:236
  237.4 3.3 copy-start.7
  240.7 4.0 %copy-start.22 = (bf16[1536,512]{1,0:T(8,128)(2,1)S(1)}, bf16[1536,512]{1,0:T(8,128)(2,1)}, u32[]{:S(2)}) copy-start(bf16[1536,512]{1,0:T(8,128)(2,1)} %get-tuple-element.25) | copy-start | bytes 4718596
  244.7 1.6 copy-start.18
  246.3 2.1 copy-start.24
  256.2 1.9 copy-start.8
  256.2 3.0 copy-start.10
  256.2 3.0 copy-start.12
  258.1 1.1 copy-start.4
  262.8 75.0 %copy-start.5 = (f32[512,512]{0,1:T(8,128)S(1)}, f32[512,512]{0,1:T(8,128)}, u32[]{:S(2)}) copy-start(f32[512,512]{0,1:T(8,128)} %copy-done.4) | copy-start | bytes 3145732
  335.8 2.1 copy-start.11
  337.9 5.5 %copy-start.15 = (f32[512,256]{1,0:T(8,128)}, f32[512,256]{1,0:T(8,128)S(1)}, u32[]{:S(2)}) copy-start(f32[512,256]{1,0:T(8,128)S(1)} %convolution_negate_fusion) | copy-start | bytes 1572868
Sparse Core Ops, SparseCore 0:
  17.1 67.4 all-reduce.2
  256.3 79.4 all-reduce.4

commit v2 on v1

v2 whole, which is shorter than its diff:
```python
import functools

import jax
import jax.numpy as jnp
from jax import lax
from jax.experimental import pallas as pl
from jax.experimental.pallas import tpu as pltpu
from jax.sharding import PartitionSpec as P

TILE = 128
MESH = pl.DeviceIdType.MESH
HIGH = lax.Precision.HIGH


def expand_mask(tile_mask):
    return jnp.repeat(jnp.repeat(tile_mask, TILE, axis=0), TILE, axis=1)


def greet(barrier, where):
    pl.semaphore_signal(barrier, inc=1, device_id=where, device_id_type=MESH)


def greet_line(barrier, chips, extra):
    row = lax.axis_index("row")
    z = lax.div(row, 2)
    greet(barrier, {"row": row + 1 - 2 * lax.rem(row, 2)})

    @pl.when(z > 0)
    def _():
        greet(barrier, {"row": row - 2})

    @pl.when(z < chips - 1)
    def _():
        greet(barrier, {"row": row + 2})

    @pl.when(jnp.logical_or(z == 0, z == chips - 1))
    def _():
        pl.semaphore_wait(barrier, 2 + extra)

    @pl.when(jnp.logical_and(z > 0, z < chips - 1))
    def _():
        pl.semaphore_wait(barrier, 3 + extra)


def landed(ref, semaphore):
    pltpu.make_async_copy(ref, ref, semaphore).wait()


def gather_kernel(chips, leaves, panel_ref, linv_ref, zero_ref, *rest):
    if leaves:
        slots, whole_panel, whole, arrivals = rest[:4]
        zrecv, zright, zleft, srecv, ssend, local, fill, lsend, lrecv = rest[4:]
    else:
        whole_panel, whole = rest[:2]
        zrecv, zright, zleft, srecv, ssend, local, fill = rest[2:]
    width = panel_ref.shape[1]
    step = 2 * width
    row = lax.axis_index("row")
    z = lax.div(row, 2)
    core = lax.rem(row, 2)
    right, left, sibling = row + 2, row - 2, row + 1 - 2 * core

    barrier = pltpu.get_barrier_semaphore()
    if leaves:
        leaf = lax.axis_index("leaf")
        for k in range(1, leaves):
            greet(barrier, {"leaf": lax.rem(leaf + k, leaves)})
    greet_line(barrier, chips, max(leaves - 1, 0))

    def place(s, c, piece):
        columns = pl.ds(pl.multiple_of((2 * s + c) * width, width), width)
        if piece == 0:
            return whole_panel.at[:, columns]
        return whole.at[pl.ds((s + piece - 1) * step, step), columns]

    def origin(s, piece):
        if piece == 0:
            return panel_ref
        return linv_ref.at[pl.ds((s + piece - 1) * step, step), :]

    def send(source, s, piece, sends, recvs, device):
        return pltpu.make_async_remote_copy(
            src_ref=source,
            dst_ref=place(s, core, piece),
            send_sem=sends.at[s, piece],
            recv_sem=recvs.at[s, piece],
            device_id={"row": device},
            device_id_type=MESH,
        )

    def pieces(s):
        return range(1 + chips - s)

    def copies(source, s, piece, go_right, go_left):
        out = []
        if go_right:
            out.append(send(source, s, piece, zright, zrecv, right))
        if go_left:
            out.append(send(source, s, piece, zleft, zrecv, left))
        out.append(send(source, s, piece, ssend, srecv, sibling))
        return out

    def own(s, piece):
        here = pltpu.make_async_copy(origin(s, piece), place(s, core, piece), local.at[piece])
        return copies(origin(s, piece), s, piece, s < chips - 1, s > 0) + [here]

    def zero_fill(s):
        return pltpu.make_async_copy(
            zero_ref.at[pl.ds(0, s * step), :],
            whole.at[pl.ds(0, s * step), pl.ds(s * step, step)],
            fill.at[s],
        )

    def across(k):
        peer = lax.rem(leaf + k, leaves)
        return pltpu.make_async_remote_copy(
            src_ref=slots.at[peer],
            dst_ref=arrivals.at[leaf],
            send_sem=lsend.at[k],
            recv_sem=lrecv.at[k],
            device_id={"leaf": peer},
            device_id_type=MESH,
        )

    for s in range(chips):
        @pl.when(z == s)
        def _(s=s):
            for piece in pieces(s):
                for copy in own(s, piece):
                    copy.start()

    if leaves:
        for k in range(1, leaves):
            across(k).start()
        keep = pltpu.make_async_copy(slots.at[leaf], arrivals.at[leaf], lsend.at[0])
        keep.start()
    for s in range(1, chips):
        zero_fill(s).start()

    def routes(hops):
        for s in range(chips):
            if s + hops < chips:
                yield s, s + hops, s + hops < chips - 1, False
            if s - hops >= 0:
                yield s, s - hops, False, s - hops > 0

    for hops in range(1, chips):
        for piece in range(chips + 1):
            for s, here, go_right, go_left in routes(hops):
                if piece in pieces(s):
                    @pl.when(z == here)
                    def _(s=s, piece=piece, go_right=go_right, go_left=go_left):
                        landed(place(s, core, piece), zrecv.at[s, piece])
                        for copy in copies(place(s, core, piece), s, piece, go_right, go_left):
                            copy.start()

    for s in range(chips):
        for piece in pieces(s):
            landed(place(s, 1 - core, piece), srecv.at[s, piece])

        @pl.when(z == s)
        def _(s=s):
            for piece in pieces(s):
                moves = own(s, piece)
                for copy in moves[:-1]:
                    copy.wait_send()
                moves[-1].wait()

    for hops in range(1, chips):
        for s, here, go_right, go_left in routes(hops):
            @pl.when(z == here)
            def _(s=s, go_right=go_right, go_left=go_left):
                for piece in pieces(s):
                    for copy in copies(place(s, core, piece), s, piece, go_right, go_left):
                        copy.wait_send()

    for s in range(1, chips):
        zero_fill(s).wait()
    if leaves:
        keep.wait()
        for k in range(1, leaves):
            across(k).wait_send()
            landed(arrivals.at[lax.rem(leaf + leaves - k, leaves)], lrecv.at[k])


def gather_block(panel, linv, chips, number, slots=None):
    order, width = linv.shape
    rows = panel.shape[0]
    step = 2 * width
    kind = linv.dtype
    any_space = pl.BlockSpec(memory_space=pl.ANY)
    shapes = [jax.ShapeDtypeStruct((rows, order), kind), jax.ShapeDtypeStruct((order, order), kind)]
    operands = [panel, linv, jnp.zeros((order - step, step), kind)]
    scratch = [pltpu.SemaphoreType.DMA((chips, chips + 1))] * 5
    scratch += [pltpu.SemaphoreType.DMA((chips + 1,)), pltpu.SemaphoreType.DMA((chips,))]
    leaves = 0
    if slots is not None:
        leaves = slots.shape[0]
        operands.append(slots)
        shapes.append(jax.ShapeDtypeStruct(slots.shape, slots.dtype))
        scratch += [pltpu.SemaphoreType.DMA((leaves,))] * 2
    moved = (rows * order + order * order) * 2
    return pl.pallas_call(
        functools.partial(gather_kernel, chips, leaves),
        out_shape=shapes,
        in_specs=[any_space] * len(operands),
        out_specs=[any_space] * len(shapes),
        scratch_shapes=scratch,
        compiler_params=pltpu.CompilerParams(collective_id=number, has_side_effects=True),
        cost_estimate=pl.CostEstimate(flops=0, bytes_accessed=moved * 20, transcendentals=0),
        name="gather_%d" % number,
    )(*operands)


CHUNKS = 4


def line_sum_kernel(chips, part_ref, out_ref, other, total, from_left, from_right, to_right, to_left, *sems):
    pair, fl, fr, sr, sl, back_send, back_recv = sems
    half = total.shape[0]
    size = half // CHUNKS
    row = lax.axis_index("row")
    z = lax.div(row, 2)
    core = lax.rem(row, 2)
    right, left, sibling = row + 2, row - 2, row + 1 - 2 * core
    greet_line(pltpu.get_barrier_semaphore(), chips, 0)

    def remote(source, target, sends, recvs, device):
        return pltpu.make_async_remote_copy(
            src_ref=source,
            dst_ref=target,
            send_sem=sends,
            recv_sem=recvs,
            device_id={"row": device},
            device_id_type=MESH,
        )

    mine = pl.ds(pl.multiple_of(core * half, half), half)
    theirs = pl.ds(pl.multiple_of((1 - core) * half, half), half)
    swap = remote(part_ref.at[theirs], other, pair.at[0], pair.at[1], sibling)
    swap.start()

    @pl.when(z == 0)
    def _():
        from_left[...] = jnp.zeros_like(from_left)

    @pl.when(z == chips - 1)
    def _():
        from_right[...] = jnp.zeros_like(from_right)

    swap.wait()
    total[...] = part_ref[mine] + other[...]

    def rightward(q):
        here = pl.ds(q * size, size)
        return remote(to_right.at[here], from_left.at[here], sr.at[q], fl.at[q], right)

    def leftward(q):
        here = pl.ds(q * size, size)
        return remote(to_left.at[here], from_right.at[here], sl.at[q], fr.at[q], left)

    def go_right():
        for q in range(CHUNKS):
            here = pl.ds(q * size, size)

            @pl.when(z > 0)
            def _(q=q, here=here):
                landed(from_left.at[here], fl.at[q])

            to_right[here] = total[here] + from_left[here]

            @pl.when(z < chips - 1)
            def _(q=q):
                rightward(q).start()

    def go_left():
        for q in range(CHUNKS):
            here = pl.ds(q * size, size)

            @pl.when(z < chips - 1)
            def _(q=q, here=here):
                landed(from_right.at[here], fr.at[q])

            to_left[here] = total[here] + from_right[here]

            @pl.when(z > 0)
            def _(q=q):
                leftward(q).start()

    @pl.when(z < chips // 2)
    def _():
        go_right()
        go_left()

    @pl.when(z >= chips // 2)
    def _():
        go_left()
        go_right()

    out_ref[mine] = to_right[...] + from_right[...]
    back = remote(out_ref.at[mine], out_ref.at[mine], back_send, back_recv, sibling)
    back.start()
    for q in range(CHUNKS):
        @pl.when(z < chips - 1)
        def _(q=q):
            rightward(q).wait_send()

        @pl.when(z > 0)
        def _(q=q):
            leftward(q).wait_send()

    back.wait_send()
    landed(out_ref.at[theirs], back_recv)


def line_sum(part, chips, number):
    rows, columns = part.shape
    half = rows // 2
    vmem = pl.BlockSpec(memory_space=pltpu.VMEM)
    chunked = pltpu.SemaphoreType.DMA((CHUNKS,))
    return pl.pallas_call(
        functools.partial(line_sum_kernel, chips),
        out_shape=jax.ShapeDtypeStruct(part.shape, part.dtype),
        in_specs=[vmem],
        out_specs=vmem,
        scratch_shapes=[pltpu.VMEM((half, columns), part.dtype)] * 6
        + [pltpu.SemaphoreType.DMA((2,))]
        + [chunked] * 4
        + [pltpu.SemaphoreType.DMA(())] * 2,
        compiler_params=pltpu.CompilerParams(
            collective_id=number, has_side_effects=True, vmem_limit_bytes=24 * 1024 * 1024
        ),
        name="line_sum",
    )(part)


def spread_tiles(selected, tile_list):
    width = selected.shape[1]
    per = width // TILE
    row = lax.axis_index("row")
    parts = []
    for a in range(tile_list.shape[0]):
        tile = tile_list[a]
        piece = jnp.zeros((selected.shape[0], TILE), selected.dtype)
        for k in range(per):
            hit = tile == row * per + k
            piece = piece + jnp.where(hit, selected[:, k * TILE:(k + 1) * TILE], 0.0)
        parts.append(piece)
    return jnp.concatenate(parts, axis=1)


def finish_block(select, whole_panel, whole, linv):
    width = linv.shape[1]
    row = lax.axis_index("row")
    across = (((0,), (0,)), ((), ()))
    upper = jnp.dot(whole_panel, whole, preferred_element_type=jnp.float32)
    gram = lax.dot_general(whole, linv, across, preferred_element_type=jnp.float32)
    own = lax.dynamic_slice_in_dim(upper, row * width, width, 1)
    cross = -jnp.dot(select, own, precision=HIGH)
    sigma = gram - lax.dot_general(upper, cross, across, precision=HIGH)
    return sigma, cross


def take_tiles(matrix, tile_list):
    return jnp.concatenate(
        [
            lax.dynamic_slice_in_dim(matrix, tile_list[a] * TILE, TILE, 0)
            for a in range(tile_list.shape[0])
        ],
        axis=0,
    )


def body(
    chips,
    sigma_root,
    linv_one,
    panel_one,
    tiles_one,
    mask_one,
    linv_two,
    panel_two,
    tiles_two,
    mask_two,
    parent,
):
    leaf_id = lax.axis_index("leaf")
    width = sigma_root.shape[1]
    own_tiles = lax.dynamic_index_in_dim(tiles_one, leaf_id, 0, keepdims=False)
    selected_first = take_tiles(sigma_root, own_tiles)
    select_first = lax.psum(spread_tiles(selected_first, own_tiles), "row")
    masked_one = panel_one[0] * expand_mask(mask_one[0]).astype(jnp.bfloat16)
    masked_two = panel_two[0] * expand_mask(mask_two[0]).astype(jnp.bfloat16)
    panel_first, whole_first = gather_block(masked_one, linv_one[0], chips, 0)
    sigma_first, cross_first = finish_block(select_first, panel_first, whole_first, linv_one[0])
    count, per_block = tiles_two.shape
    owned = (parent == leaf_id).astype(jnp.float32)
    slots = take_tiles(sigma_first, tiles_two.reshape(-1)).reshape(count, per_block * TILE, width)
    slots = slots * owned[:, None, None]
    panel_second, whole_second, arrived = gather_block(masked_two, linv_two[0], chips, 1, slots)
    tiles_second = lax.dynamic_index_in_dim(tiles_two, leaf_id, 0, keepdims=False)
    spread = spread_tiles(jnp.sum(arrived, axis=0), tiles_second)
    select_second = line_sum(spread, chips, 2)
    sigma_second, cross_second = finish_block(select_second, panel_second, whole_second, linv_two[0])
    return (sigma_first[None], cross_first[None], sigma_second[None], cross_second[None])


def solution(mesh):
    chips = mesh.shape["row"] // 2
    return jax.shard_map(
        functools.partial(body, chips),
        mesh=mesh,
        in_specs=(
            P(None, "row"),
            P("leaf", None, "row"),
            P("leaf", None, "row"),
            P(),
            P("leaf", None, "row"),
            P("leaf", None, "row"),
            P("leaf", None, "row"),
            P(),
            P("leaf", None, "row"),
            P(),
        ),
        out_specs=(
            P("leaf", None, "row"),
            P("leaf", None, "row"),
            P("leaf", None, "row"),
            P("leaf", None, "row"),
        ),
        check_vma=False,
    )
```

time: 351 us -> 418 us (1.19)
  Pallas kernels: 146 us -> 325 us
  waiting for transfers between devices: 91.1 us -> 0.04 us
  other arithmetic: 19.6 us -> 6.23 us
  between operations: 24.9 us -> 37.6 us
  local copies, waits for them, and re-layouts: 15.8 us -> 7.87 us
  matrix products: 48.2 us -> 40.4 us
  starting transfers between devices: 4.65 us -> 0.04 us
    pallas_call x2 -> x3, Pallas kernels: 146 us -> 325 us  [the longest x2 296 us: gather_block(): pl.pallas_call(functools.partial(gather_kernel, chips, leaves), out_shape...]
    psum x1 -> x0, waiting for transfers between devices: 72.9 us -> none  [body(): select_second = lax.psum(spread_tiles(selected_second, tiles_second), 'row')]
    all_to_all x1 -> x0, waiting for transfers between devices: 18.2 us -> none  [body(): lax.all_to_all(slots, 'leaf', split_axis=0, concat_axis=0, tiled=True)]
    gather x2 -> x0, local copies, waits for them, and re-layouts: 11.8 us -> none  [the longest x1 10.2 us: body(): jnp.take(sigma_first, rows_every.reshape(-1), axis=0)]
    concatenate x2 -> x1, other arithmetic: 8.21 us -> 0.04 us  [take_tiles(): jnp.concatenate([lax.dynamic_slice_in_dim(matrix, tile_list[a] * TILE, TI...]
    dot_general x18 -> x6, matrix products: 44 us -> 37.8 us  [the longest x2 15.1 us: finish_block(): upper = jnp.dot(whole_panel, whole, preferred_element_type=jnp.float32)]
    all_to_all x1 -> x0, starting transfers between devices: 4.57 us -> none  [body(): lax.all_to_all(slots, 'leaf', split_axis=0, concat_axis=0, tiled=True)]
  transfers between devices with their start and end apart: 3 -> 1, of which waited for: 2 -> 0; matrix products, arithmetic and copies ran while one was open for 9% -> 5% of each run, Pallas kernels for 22% -> 34%
where the time goes in v2:
time: 418 us
  Pallas kernels  325 us (78%)
  matrix products  40.4 us (10%)
  between operations  37.6 us (9%)
  local copies, waits for them, and re-layouts  7.87 us (2%)
  other arithmetic  6.23 us (1%)
    pallas_call x2, Pallas kernels, gather_block(): pl.pallas_call(functools.partial(gather_kernel, chips, leaves), out_shape...  296 us
    pallas_call x1, Pallas kernels, line_sum(): pl.pallas_call(functools.partial(line_sum_kernel, chips), out_shape=jax.S...  29.8 us
    dot_general x2, matrix products, finish_block(): upper = jnp.dot(whole_panel, whole, preferred_element_type=jnp.float32)  15.1 us
    dot_general x2, matrix products, finish_block(): lax.dot_general(whole, linv, across, preferred_element_type=jnp.float32)  12 us
    dot_general x2, matrix products, finish_block(): sigma = gram - lax.dot_general(upper, cross, across, precision=HIGH)  10.7 us
  transfers between devices with their start and end apart: 1, of which 0 were waited for; matrix products, arithmetic and copies ran while one was open for 5% of the time, Pallas kernels for 34%

profile of v2, /device:TPU:0, one launch (start us, length us, event | category | flops | bytes accessed | tf_op | source)
XLA Modules:
  0.0 417.5 jit_solution(10487320580155848226)
XLA Ops:
  7.2 0.0 all-reduce.2.cloned.1.call-start
  7.2 0.7 constant_dynamic-slice_fusion
  7.9 0.6 fusion.11
  16.3 1.1 constant_dynamic-slice_fusion.4
  17.6 0.1 select_add_fusion.7
  17.7 1.0 pad_maximum_fusion
  18.8 0.1 reshape.73
  18.9 0.7 fusion.10
  29.8 0.7 fusion.9
  35.5 0.1 copy.14
  35.7 0.1 copy.15
  35.8 0.6 broadcast_in_dim.45
  36.4 0.8 bitcast_multiply_fusion.1.panel_ref
  37.2 1.2 broadcast_1_zero_ref.2.zero_ref
  38.4 140.1 %gather_0.1 = (bf16[512,2048]{1,0:T(8,128)(2,1)}, bf16[2048,2048]{1,0:T(8,128)(2,1)}) custom-call(bf16[512,256]{1,0:T(8,128)(2,1)} %bitcast_multiply_fusion.1.panel_ref, bf16[2048,256]{1,0:T(8,128)(2,1)} %bitcast.71, bf16[1536,512]{1,0:T(8,128)(2,1)} %broadcast_1_zero_ref.2.zero_ref), custom_call_target="tpu_custom_call" | custom-call | bytes 209715200 | tf_op jit(solution)/shard_map/gather_0/pallas_call | solution.py:203
  178.6 10.6 %fusion.12 = f32[512,2048]{1,0:T(8,128)} fusion(bf16[512,2048]{1,0:T(8,128)(2,1)} %get-tuple-element.10, bf16[2048,2048]{1,0:T(8,128)(2,1)} %get-tuple-element.9), kind=kOutput, calls=%fused_computation.55 | convolution fusion | flops 4294967296 | bytes 14680064 | tf_op jit(solution)/shard_map/dot_general | solution.py:356
  189.2 0.6 broadcast_in_dim.50
  189.8 0.8 bitcast_multiply_fusion.panel_ref
  190.5 6.0 %fusion.7 = f32[2048,256]{1,0:T(8,128)S(1)} fusion(bf16[2048,2048]{1,0:T(8,128)(2,1)} %get-tuple-element.9, bf16[1,2048,256]{2,1,0:T(8,128)(2,1)S(1)} %copy-done.4), kind=kOutput, calls=%fused_computation.50 | convolution fusion | flops 2147483648 | bytes 11534336 | tf_op jit(solution)/shard_map/dot_general | solution.py:357
  196.6 2.0 convolution_negate_fusion.1
  198.6 6.0 %convolution_subtract_fusion.1 = f32[2048,256]{1,0:T(8,128)S(1)} fusion(f32[2048,256]{1,0:T(8,128)S(1)} %fusion.7, f32[512,2048]{1,0:T(8,128)} %fusion.12, f32[512,256]{1,0:T(8,128)S(1)} %convolution_negate_fusion.1), kind=kOutput, calls=%fused_computation.2 | convolution fusion | flops 1611137024 | bytes 8912896 | tf_op jit(solution)/shard_map/dot_general | solution.py:360
  205.0 0.9 copy-done
  205.9 1.6 broadcast_multiply_fusion.rest_0_
  207.4 155.5 %gather_1.1 = (bf16[512,2048]{1,0:T(8,128)(2,1)}, bf16[2048,2048]{1,0:T(8,128)(2,1)}, f32[4,512,256]{2,1,0:T(8,128)}) custom-call(bf16[512,256]{1,0:T(8,128)(2,1)} %bitcast_multiply_fusion.panel_ref, bf16[2048,256]{1,0:T(8,128)(2,1)} %bitcast.68, bf16[1536,512]{1,0:T(8,128)(2,1)} %broadcast_1_zero_ref.2.zero_ref, f32[4,512,256]{2,1,0:T(8,128)} %broadcast_multiply_fusion.rest_0_), custom_call_target="tpu_custom_call" | custom-call | bytes 209715200 | tf_op jit(solution)/shard_map/gather_1/pallas_call | solution.py:203
  362.9 1.8 reduce_sum.9
  364.7 0.1 select_add_fusion.3
  364.8 0.1 pad_maximum_fusion.1.part_ref
  364.9 29.8 %line_sum.1 = f32[512,512]{1,0:T(8,128)S(1)} custom-call(f32[512,512]{1,0:T(8,128)S(1)} %pad_maximum_fusion.1.part_ref), custom_call_target="tpu_custom_call" | custom-call | tf_op jit(solution)/shard_map/line_sum/pallas_call | solution.py:321
  394.7 6.0 %fusion.5 = f32[2048,256]{1,0:T(8,128)S(1)} fusion(bf16[2048,2048]{1,0:T(8,128)(2,1)} %get-tuple-element.11, bf16[1,2048,256]{2,1,0:T(8,128)(2,1)S(1)} %copy-done.3), kind=kOutput, calls=%fused_computation.48 | convolution fusion | flops 2147483648 | bytes 11534336 | tf_op jit(solution)/shard_map/dot_general | solution.py:357
  400.8 4.5 %fusion.13 = f32[512,2048]{1,0:T(8,128)S(1)} fusion(bf16[512,2048]{1,0:T(8,128)(2,1)S(1)} %copy-done.8, bf16[2048,2048]{1,0:T(8,128)(2,1)S(1)} %bitcast.75), kind=kOutput, calls=%fused_computation.56 | convolution fusion | flops 4294967296 | bytes 14680064 | tf_op jit(solution)/shard_map/dot_general | solution.py:356
  405.3 0.6 convolution_negate_fusion
  405.9 4.8 %fusion = f32[1,2048,256]{2,1,0:T(8,128)} fusion(f32[2048,256]{1,0:T(8,128)S(1)} %fusion.5, f32[512,2048]{1,0:T(8,128)S(1)} %fusion.13, f32[512,256]{1,0:T(8,128)S(1)} %convolution_negate_fusion), kind=kOutput, calls=%fused_computation.1 | convolution fusion | flops 1611137024 | bytes 8912896 | tf_op jit(solution)/shard_map/dot_general | solution.py:360
  (52 shorter events, 0.5 us)
Async XLA Ops:
  7.2 189.4 %all-reduce.2.cloned.1.call-start = ((), (), s32[]{:S(2)}) async-start(), calls=%async_computation | async-start | bytes 2097152 | tf_op jit(solution)/shard_map/psum | solution.py:391
  17.5 1.3 copy-start.7
  17.5 18.0 %copy-start.9 = (s32[1,4,2]{1,2,0:T(2,128)S(1)}, s32[1,4,2]{1,2,0:T(2,128)}, u32[]{:S(2)}) copy-start(s32[1,4,2]{1,2,0:T(2,128)} %param.14) | copy-start | bytes 100
  17.5 18.1 %copy-start.11 = (s32[4]{0:T(128)S(1)}, s32[4]{0:T(128)}, u32[]{:S(2)}) copy-start(s32[4]{0:T(128)} %param.19) | copy-start | bytes 52
  17.6 18.1 %copy-start.10 = (s32[1,4,2]{1,2,0:T(2,128)S(1)}, s32[1,4,2]{1,2,0:T(2,128)}, u32[]{:S(2)}) copy-start(s32[1,4,2]{1,2,0:T(2,128)} %param.18) | copy-start | bytes 100
  17.7 18.7 %copy-start.5 = (bf16[1,512,256]{2,1,0:T(8,128)(2,1)S(1)}, bf16[1,512,256]{2,1,0:T(8,128)(2,1)}, u32[]{:S(2)}) copy-start(bf16[1,512,256]{2,1,0:T(8,128)(2,1)} %param.12) | copy-start | bytes 786436
  178.5 11.2 %copy-start.6 = (bf16[1,512,256]{2,1,0:T(8,128)(2,1)S(1)}, bf16[1,512,256]{2,1,0:T(8,128)(2,1)}, u32[]{:S(2)}) copy-start(bf16[1,512,256]{2,1,0:T(8,128)(2,1)} %param.16) | copy-start | bytes 786436
  178.6 12.0 %copy-start.4 = (bf16[1,2048,256]{2,1,0:T(8,128)(2,1)S(1)}, bf16[1,2048,256]{2,1,0:T(8,128)(2,1)}, u32[]{:S(2)}) copy-start(bf16[1,2048,256]{2,1,0:T(8,128)(2,1)} %param.11) | copy-start | bytes 3145732
  198.6 6.0 %copy-start.1 = (f32[512,256]{1,0:T(8,128)}, f32[512,256]{1,0:T(8,128)S(1)}, u32[]{:S(2)}) copy-start(f32[512,256]{1,0:T(8,128)S(1)} %convolution_negate_fusion.1) | copy-start | bytes 1572868
  204.5 1.3 copy-start
  364.8 29.9 %copy-start.3 = (bf16[1,2048,256]{2,1,0:T(8,128)(2,1)S(1)}, bf16[1,2048,256]{2,1,0:T(8,128)(2,1)}, u32[]{:S(2)}) copy-start(bf16[1,2048,256]{2,1,0:T(8,128)(2,1)} %param.15) | copy-start | bytes 3145732
  364.9 35.9 %slice-start = ((s8[8388608]{0:T(1024)(128)(4,1)}), s8[4194304]{0:T(1024)(128)(4,1)S(1)}, s32[]{:S(2)}) async-start(s8[8388608]{0:T(1024)(128)(4,1)} %bitcast.74), calls=%async_computation.1 | async-start | bytes 8388608
  394.7 6.0 %slice-start.1 = ((s8[8388608]{0:T(1024)(128)(4,1)}), s8[4194304]{0:T(1024)(128)(4,1)S(1)}, s32[]{:S(2)}) async-start(s8[8388608]{0:T(1024)(128)(4,1)} %bitcast.74), calls=%async_computation.2 | async-start | bytes 8388608
  394.7 6.0 %copy-start.8 = (bf16[512,2048]{1,0:T(8,128)(2,1)S(1)}, bf16[512,2048]{1,0:T(8,128)(2,1)}, u32[]{:S(2)}) copy-start(bf16[512,2048]{1,0:T(8,128)(2,1)} %get-tuple-element.12) | copy-start | bytes 6291460
  405.9 4.8 %copy-start.2 = (f32[512,256]{1,0:T(8,128)}, f32[512,256]{1,0:T(8,128)S(1)}, u32[]{:S(2)}) copy-start(f32[512,256]{1,0:T(8,128)S(1)} %convolution_negate_fusion) | copy-start | bytes 1572868
Sparse Core Ops, SparseCore 0:
  18.9 66.1 all-reduce.1

commit v3 on v2

--- a/solution.py
+++ b/solution.py
@@ -46,13 +46,14 @@
     pltpu.make_async_copy(ref, ref, semaphore).wait()
 
 
-def gather_kernel(chips, leaves, panel_ref, linv_ref, zero_ref, *rest):
+def gather_kernel(chips, leaves, panel_ref, linv_ref, *rest):
     if leaves:
-        slots, whole_panel, whole, arrivals = rest[:4]
-        zrecv, zright, zleft, srecv, ssend, local, fill, lsend, lrecv = rest[4:]
-    else:
-        whole_panel, whole = rest[:2]
-        zrecv, zright, zleft, srecv, ssend, local, fill = rest[2:]
+        slots, rest = rest[0], rest[1:]
+    whole_panel, blocks, rest = rest[0], rest[1:chips + 1], rest[chips + 1:]
+    if leaves:
+        arrivals, lsend, lrecv = rest[0], rest[-2], rest[-1]
+        rest = rest[1:-2]
+    zrecv, zright, zleft, srecv, ssend, local = rest
     width = panel_ref.shape[1]
     step = 2 * width
     row = lax.axis_index("row")
@@ -68,10 +69,9 @@
     greet_line(barrier, chips, max(leaves - 1, 0))
 
     def place(s, c, piece):
-        columns = pl.ds(pl.multiple_of((2 * s + c) * width, width), width)
         if piece == 0:
-            return whole_panel.at[:, columns]
-        return whole.at[pl.ds((s + piece - 1) * step, step), columns]
+            return whole_panel.at[2 * s + c]
+        return blocks[s].at[c, pl.ds((piece - 1) * step, step), :]
 
     def origin(s, piece):
         if piece == 0:
@@ -103,13 +103,6 @@
     def own(s, piece):
         here = pltpu.make_async_copy(origin(s, piece), place(s, core, piece), local.at[piece])
         return copies(origin(s, piece), s, piece, s < chips - 1, s > 0) + [here]
-
-    def zero_fill(s):
-        return pltpu.make_async_copy(
-            zero_ref.at[pl.ds(0, s * step), :],
-            whole.at[pl.ds(0, s * step), pl.ds(s * step, step)],
-            fill.at[s],
-        )
 
     def across(k):
         peer = lax.rem(leaf + k, leaves)
@@ -134,8 +127,6 @@
             across(k).start()
         keep = pltpu.make_async_copy(slots.at[leaf], arrivals.at[leaf], lsend.at[0])
         keep.start()
-    for s in range(1, chips):
-        zero_fill(s).start()
 
     def routes(hops):
         for s in range(chips):
@@ -174,8 +165,6 @@
                     for copy in copies(place(s, core, piece), s, piece, go_right, go_left):
                         copy.wait_send()
 
-    for s in range(1, chips):
-        zero_fill(s).wait()
     if leaves:
         keep.wait()
         for k in range(1, leaves):
@@ -189,10 +178,11 @@
     step = 2 * width
     kind = linv.dtype
     any_space = pl.BlockSpec(memory_space=pl.ANY)
-    shapes = [jax.ShapeDtypeStruct((rows, order), kind), jax.ShapeDtypeStruct((order, order), kind)]
-    operands = [panel, linv, jnp.zeros((order - step, step), kind)]
+    shapes = [jax.ShapeDtypeStruct((2 * chips, rows, width), kind)]
+    shapes += [jax.ShapeDtypeStruct((2, order - s * step, width), kind) for s in range(chips)]
+    operands = [panel, linv]
     scratch = [pltpu.SemaphoreType.DMA((chips, chips + 1))] * 5
-    scratch += [pltpu.SemaphoreType.DMA((chips + 1,)), pltpu.SemaphoreType.DMA((chips,))]
+    scratch += [pltpu.SemaphoreType.DMA((chips + 1,))]
     leaves = 0
     if slots is not None:
         leaves = slots.shape[0]
@@ -200,7 +190,7 @@
         shapes.append(jax.ShapeDtypeStruct(slots.shape, slots.dtype))
         scratch += [pltpu.SemaphoreType.DMA((leaves,))] * 2
     moved = (rows * order + order * order) * 2
-    return pl.pallas_call(
+    out = pl.pallas_call(
         functools.partial(gather_kernel, chips, leaves),
         out_shape=shapes,
         in_specs=[any_space] * len(operands),
@@ -210,6 +200,8 @@
         cost_estimate=pl.CostEstimate(flops=0, bytes_accessed=moved * 20, transcendentals=0),
         name="gather_%d" % number,
     )(*operands)
+    arrived = out[chips + 1] if leaves else None
+    return out[0], out[1:chips + 1], arrived
 
 
 CHUNKS = 4
@@ -349,15 +341,25 @@
     return jnp.concatenate(parts, axis=1)
 
 
-def finish_block(select, whole_panel, whole, linv):
+def finish_block(select, panels, blocks, linv):
     width = linv.shape[1]
     row = lax.axis_index("row")
     across = (((0,), (0,)), ((), ()))
-    upper = jnp.dot(whole_panel, whole, preferred_element_type=jnp.float32)
-    gram = lax.dot_general(whole, linv, across, preferred_element_type=jnp.float32)
+    whole_panel = jnp.concatenate([panels[r] for r in range(panels.shape[0])], axis=1)
+    upper, gram = [], []
+    for s, pair in enumerate(blocks):
+        start = 2 * s * width
+        for c in range(2):
+            upper.append(
+                jnp.dot(whole_panel[:, start:], pair[c], preferred_element_type=jnp.float32)
+            )
+            gram.append(
+                lax.dot_general(pair[c], linv[start:], across, preferred_element_type=jnp.float32)
+            )
+    upper = jnp.concatenate(upper, axis=1)
     own = lax.dynamic_slice_in_dim(upper, row * width, width, 1)
     cross = -jnp.dot(select, own, precision=HIGH)
-    sigma = gram - lax.dot_general(upper, cross, across, precision=HIGH)
+    sigma = jnp.concatenate(gram, axis=0) - lax.dot_general(upper, cross, across, precision=HIGH)
     return sigma, cross
 
 
@@ -391,7 +393,7 @@
     select_first = lax.psum(spread_tiles(selected_first, own_tiles), "row")
     masked_one = panel_one[0] * expand_mask(mask_one[0]).astype(jnp.bfloat16)
     masked_two = panel_two[0] * expand_mask(mask_two[0]).astype(jnp.bfloat16)
-    panel_first, whole_first = gather_block(masked_one, linv_one[0], chips, 0)
+    panel_first, whole_first, _ = gather_block(masked_one, linv_one[0], chips, 0)
     sigma_first, cross_first = finish_block(select_first, panel_first, whole_first, linv_one[0])
     count, per_block = tiles_two.shape
     owned = (parent == leaf_id).astype(jnp.float32)

time: 418 us -> 297 us (0.71)
  Pallas kernels: 325 us -> 194 us
  local copies, waits for them, and re-layouts: 7.87 us -> 24.9 us
  matrix products: 40.4 us -> 32.9 us
    pallas_call x2, Pallas kernels: 296 us -> 147 us  [gather_block(): pl.pallas_call(functools.partial(gather_kernel, chips, leaves), out_shape...]
    pallas_call x1, Pallas kernels: 29.8 us -> 47.1 us  [line_sum(): pl.pallas_call(functools.partial(line_sum_kernel, chips), out_shape=jax.S...]
    unnamed x43 -> x87, local copies, waits for them, and re-layouts: 1.25 us -> 15.4 us
    dot_general x6 -> x34, matrix products: 37.8 us -> 30.3 us  [the longest x16 13.4 us: finish_block(): lax.dot_general(pair[c], linv[start:], across, preferred_element_type=jnp...]
  transfers between devices with their start and end apart: 1 -> 1, of which waited for: 0 -> 0; matrix products, arithmetic and copies ran while one was open for 5% -> 9% of each run, Pallas kernels for 34% -> 26%
where the time goes in v3:
time: 297 us; the launch traced here: 295 us
  Pallas kernels  194 us (65%)
  between operations  37.8 us (13%)
  matrix products  32.9 us (11%)
  local copies, waits for them, and re-layouts  24.9 us (8%)
  other arithmetic  4.65 us (2%)
    pallas_call x2, Pallas kernels, gather_block(): pl.pallas_call(functools.partial(gather_kernel, chips, leaves), out_shape...  147 us
    pallas_call x1, Pallas kernels, line_sum(): pl.pallas_call(functools.partial(line_sum_kernel, chips), out_shape=jax.S...  47.1 us
    unnamed x87, local copies, waits for them, and re-layouts  15.4 us
    dot_general x16, matrix products, finish_block(): lax.dot_general(pair[c], linv[start:], across, preferred_element_type=jnp...  13.4 us
    dot_general x16, matrix products, finish_block(): jnp.dot(whole_panel[:, start:], pair[c], preferred_element_type=jnp.float32)  8.82 us
    dot_general x2, matrix products, finish_block(): lax.dot_general(upper, cross, across, precision=HIGH)  8.05 us
  transfers between devices with their start and end apart: 1, of which 0 were waited for; matrix products, arithmetic and copies ran while one was open for 9% of the time, Pallas kernels for 26%

profile of v3, /device:TPU:0, one launch (start us, length us, event | category | flops | bytes accessed | tf_op | source)
XLA Modules:
  0.0 294.7 jit_solution(13008161016519260183)
XLA Ops:
  16.3 1.1 constant_dynamic-slice_fusion.4
  17.7 1.1 pad_maximum_fusion.1
  19.6 0.7 bitcast_multiply_fusion.1.panel_ref
  20.3 78.0 %gather_0.1 = (bf16[8,512,256]{2,1,0:T(8,128)(2,1)}, bf16[2,2048,256]{2,1,0:T(8,128)(2,1)}, bf16[2,1536,256]{2,1,0:T(8,128)(2,1)}, bf16[2,1024,256]{2,1,0:T(8,128)(2,1)}, bf16[2,512,256]{2,1,0:T(8,128)(2,1)}) custom-call(bf16[512,256]{1,0:T(8,128)(2,1)} %bitcast_multiply_fusion.1.panel_ref, bf16[2048,256]{1,0:T(8,128)(2,1)} %bitcast.248), custom_call_target="tpu_custom_call" | custom-call | bytes 209715200 | tf_op jit(solution)/shard_map/gather_0/pallas_call | solution.py:193
  98.4 1.8 bitcast_dynamic-update-slice_fusion.11
  100.2 2.1 slice_bitcast_fusion.7
  102.3 1.7 bitcast_dynamic-update-slice_fusion.10
  104.0 0.7 bitcast_dynamic-update-slice_fusion.8
  104.8 2.5 convolution_dynamic-update-slice_fusion.31
  107.6 1.3 copy-done.9
  108.9 0.8 convolution_dynamic-update-slice_fusion.7
  109.7 0.8 convolution_dynamic-update-slice_fusion.6
  115.4 1.6 convolution_dynamic-update-slice_fusion.30
  117.0 1.1 convolution_dynamic-update-slice_fusion.29
  118.1 1.1 convolution_dynamic-update-slice_fusion.28
  119.2 1.0 convolution_dynamic-update-slice_fusion.27
  120.3 1.0 convolution_dynamic-update-slice_fusion.26
  121.3 1.0 convolution_dynamic-update-slice_fusion.25
  138.9 1.0 convolution_dynamic-update-slice_fusion.24
  140.5 0.7 bitcast_multiply_fusion.panel_ref
  141.3 2.0 convolution_negate_fusion.1
  143.3 4.9 %convolution_subtract_fusion.1 = f32[2048,256]{1,0:T(8,128)S(1)} fusion(f32[2048,256]{1,0:T(8,128)} %convolution_dynamic-update-slice_fusion.24, f32[512,2048]{0,1:T(8,128)} %copy-done.3, f32[512,256]{1,0:T(8,128)S(1)} %convolution_negate_fusion.1), kind=kOutput, calls=%fused_computation.2 | convolution fusion | flops 1611137024 | bytes 8912896 | tf_op jit(solution)/shard_map/dot_general | solution.py:362
  148.6 0.9 copy-done.2
  149.5 1.6 broadcast_multiply_fusion.rest_0_
  151.1 69.4 %gather_1.1 = (bf16[8,512,256]{2,1,0:T(8,128)(2,1)}, bf16[2,2048,256]{2,1,0:T(8,128)(2,1)}, bf16[2,1536,256]{2,1,0:T(8,128)(2,1)}, bf16[2,1024,256]{2,1,0:T(8,12...) custom-call(bf16[512,256]{1,0:T(8,128)(2,1)} %bitcast_multiply_fusion.panel_ref, ...), custom_call_target="tpu_custom_call" | custom-call | bytes 209715200 | tf_op jit(solution)/shard_map/gather_1/pallas_call | solution.py:193
  220.5 1.8 bitcast_dynamic-update-slice_fusion.5
  222.3 2.0 slice_bitcast_fusion.3
  224.7 47.1 %line_sum.1 = f32[512,512]{1,0:T(8,128)S(1)} custom-call(f32[512,512]{1,0:T(8,128)S(1)} %pad_maximum_fusion.3.part_ref), custom_call_target="tpu_custom_call" | custom-call | tf_op jit(solution)/shard_map/line_sum/pallas_call | solution.py:313
  273.7 1.1 copy-done.17
  275.1 0.8 convolution_dynamic-update-slice_fusion.3
  275.9 0.8 convolution_dynamic-update-slice_fusion.2
  284.7 3.1 %fusion = f32[1,2048,256]{2,1,0:T(8,128)} fusion(f32[2048,256]{1,0:T(8,128)S(1)} %convolution_dynamic-update-slice_fusion.16, f32[512,2048]{0,1:T(8,128)S(1)} %convolution_dynamic-update-slice_fusion.8, f32[512,256]{1,0:T(8,128)S(1)} %convolution_negate_fusion), kind=kOutput, calls=%fused_computation.1 | convolution fusion | flops 1611137024 | bytes 8912896 | tf_op jit(solution)/shard_map/dot_general | solution.py:362
  (126 shorter events, 20.3 us)
Async XLA Ops:
  7.2 134.1 %all-reduce.2.cloned.1.call-start = ((), (), s32[]{:S(2)}) async-start(), calls=%async_computation | async-start | bytes 2097152 | tf_op jit(solution)/shard_map/psum | solution.py:393
  17.5 1.3 copy-start.26
  17.6 1.9 copy-start.11
  20.3 82.0 %copy-start.19 = (s32[4,4]{1,0:T(4,128)S(1)}, s32[4,4]{1,0:T(4,128)}, u32[]{:S(2)}) copy-start(s32[4,4]{1,0:T(4,128)} %param.17) | copy-start | bytes 196
  98.3 5.7 %copy-start.5 = (bf16[8,512,256]{2,1,0:T(8,128)(2,1)S(1)}, bf16[8,512,256]{2,1,0:T(8,128)(2,1)}, u32[]{:S(2)}) copy-start(bf16[8,512,256]{2,1,0:T(8,128)(2,1)} %get-tuple-element.19) | copy-start | bytes 6291460
  98.3 6.4 %copy-start = (bf16[1,2048,256]{2,1,0:T(8,128)(2,1)S(1)}, bf16[1,2048,256]{2,1,0:T(8,128)(2,1)}, u32[]{:S(2)}) copy-start(bf16[1,2048,256]{2,1,0:T(8,128)(2,1)} %param.11) | copy-start | bytes 3145732
  104.8 2.6 copy-start.18
  107.3 1.6 copy-start.9
  109.7 1.4 copy-start.21
  111.7 1.0 copy-start.14
  111.7 1.0 copy-start.15
  111.7 1.1 copy-start.16
  111.7 1.4 copy-start.23
  113.7 1.0 copy-start.24
  115.4 2.7 copy-start.3
  119.2 3.8 %copy-start.28 = (s32[4]{0:T(128)S(1)}, s32[4]{0:T(128)}, u32[]{:S(2)}) copy-start(s32[4]{0:T(128)} %param.19) | copy-start | bytes 52
  119.2 3.8 %copy-start.27 = (s32[1,4,2]{1,2,0:T(2,128)S(1)}, s32[1,4,2]{1,2,0:T(2,128)}, u32[]{:S(2)}) copy-start(s32[1,4,2]{1,2,0:T(2,128)} %param.18) | copy-start | bytes 100
  120.2 20.3 %copy-start.12 = (bf16[1,512,256]{2,1,0:T(8,128)(2,1)S(1)}, bf16[1,512,256]{2,1,0:T(8,128)(2,1)}, u32[]{:S(2)}) copy-start(bf16[1,512,256]{2,1,0:T(8,128)(2,1)} %param.16) | copy-start | bytes 786436
  143.3 4.9 %copy-start.6 = (f32[512,256]{1,0:T(8,128)}, f32[512,256]{1,0:T(8,128)S(1)}, u32[]{:S(2)}) copy-start(f32[512,256]{1,0:T(8,128)S(1)} %convolution_negate_fusion.1) | copy-start | bytes 1572868
  148.2 1.3 copy-start.2
  220.5 3.8 %copy-start.10 = (f32[4,512,256]{2,1,0:T(8,128)S(1)}, f32[4,512,256]{2,1,0:T(8,128)}, u32[]{:S(2)}) copy-start(f32[4,512,256]{2,1,0:T(8,128)} %get-tuple-element.25) | copy-start | bytes 6291460
  224.6 47.2 %copy-start.4 = (bf16[8,512,256]{2,1,0:T(8,128)(2,1)S(1)}, bf16[8,512,256]{2,1,0:T(8,128)(2,1)}, u32[]{:S(2)}) copy-start(bf16[8,512,256]{2,1,0:T(8,128)(2,1)} %get-tuple-element.24) | copy-start | bytes 6291460
  224.7 48.6 %copy-start.1 = (bf16[1,2048,256]{2,1,0:T(8,128)(2,1)S(1)}, bf16[1,2048,256]{2,1,0:T(8,128)(2,1)}, u32[]{:S(2)}) copy-start(bf16[1,2048,256]{2,1,0:T(8,128)(2,1)} %param.15) | copy-start | bytes 3145732
  224.7 48.6 %copy-start.8 = (bf16[2,2048,256]{2,1,0:T(8,128)(2,1)S(1)}, bf16[2,2048,256]{2,1,0:T(8,128)(2,1)}, u32[]{:S(2)}) copy-start(bf16[2,2048,256]{2,1,0:T(8,128)(2,1)} %get-tuple-element.20) | copy-start | bytes 6291460
  273.2 1.6 copy-start.17
  275.9 1.4 copy-start.20
  277.9 1.0 copy-start.13
  277.9 1.3 copy-start.22
  279.7 1.0 copy-start.25
  284.7 3.2 %copy-start.7 = (f32[512,256]{1,0:T(8,128)}, f32[512,256]{1,0:T(8,128)S(1)}, u32[]{:S(2)}) copy-start(f32[512,256]{1,0:T(8,128)S(1)} %convolution_negate_fusion) | copy-start | bytes 1572868
Sparse Core Ops, SparseCore 0:
  18.9 67.4 all-reduce.1

commit v4 on v3

--- a/solution.py
+++ b/solution.py
@@ -70,8 +70,8 @@
 
     def place(s, c, piece):
         if piece == 0:
-            return whole_panel.at[2 * s + c]
-        return blocks[s].at[c, pl.ds((piece - 1) * step, step), :]
+            return whole_panel.at[:, pl.ds(pl.multiple_of((2 * s + c) * width, width), width)]
+        return blocks[s].at[pl.ds((piece - 1) * step, step), pl.ds(pl.multiple_of(c * width, width), width)]
 
     def origin(s, piece):
         if piece == 0:
@@ -178,8 +178,8 @@
     step = 2 * width
     kind = linv.dtype
     any_space = pl.BlockSpec(memory_space=pl.ANY)
-    shapes = [jax.ShapeDtypeStruct((2 * chips, rows, width), kind)]
-    shapes += [jax.ShapeDtypeStruct((2, order - s * step, width), kind) for s in range(chips)]
+    shapes = [jax.ShapeDtypeStruct((rows, order), kind)]
+    shapes += [jax.ShapeDtypeStruct((order - s * step, step), kind) for s in range(chips)]
     operands = [panel, linv]
     scratch = [pltpu.SemaphoreType.DMA((chips, chips + 1))] * 5
     scratch += [pltpu.SemaphoreType.DMA((chips + 1,))]
@@ -341,25 +341,29 @@
     return jnp.concatenate(parts, axis=1)
 
 
-def finish_block(select, panels, blocks, linv):
+def finish_block(select, whole_panel, blocks, linv):
     width = linv.shape[1]
+    step = 2 * width
     row = lax.axis_index("row")
-    across = (((0,), (0,)), ((), ()))
-    whole_panel = jnp.concatenate([panels[r] for r in range(panels.shape[0])], axis=1)
-    upper, gram = [], []
-    for s, pair in enumerate(blocks):
-        start = 2 * s * width
-        for c in range(2):
-            upper.append(
-                jnp.dot(whole_panel[:, start:], pair[c], preferred_element_type=jnp.float32)
-            )
-            gram.append(
-                lax.dot_general(pair[c], linv[start:], across, preferred_element_type=jnp.float32)
-            )
-    upper = jnp.concatenate(upper, axis=1)
+    upper = jnp.concatenate(
+        [
+            jnp.dot(whole_panel[:, s * step:], block, preferred_element_type=jnp.float32)
+            for s, block in enumerate(blocks)
+        ],
+        axis=1,
+    )
     own = lax.dynamic_slice_in_dim(upper, row * width, width, 1)
     cross = -jnp.dot(select, own, precision=HIGH)
-    sigma = jnp.concatenate(gram, axis=0) - lax.dot_general(upper, cross, across, precision=HIGH)
+    gram = jnp.concatenate(
+        [
+            lax.dot_general(
+                block, linv[s * step:], (((0,), (0,)), ((), ())), preferred_element_type=jnp.float32
+            )
+            for s, block in enumerate(blocks)
+        ],
+        axis=0,
+    )
+    sigma = gram - lax.dot_general(upper, cross, (((0,), (0,)), ((), ())), precision=HIGH)
     return sigma, cross
 
 

time: 297 us -> 286 us (0.963)
  local copies, waits for them, and re-layouts: 24.9 us -> 7.76 us
  matrix products: 32.9 us -> 40.1 us
  Pallas kernels: 194 us -> 187 us
  other arithmetic: 4.65 us -> 10.6 us
    unnamed x87 -> x73, local copies, waits for them, and re-layouts: 15.4 us -> 2.45 us
    dot_general x34 -> x18, matrix products: 30.3 us -> 37.4 us  [the longest x8 14.6 us: finish_block(): jnp.dot(whole_panel[:, s * step:], block, preferred_element_type=jnp.floa...]
    pallas_call x2, Pallas kernels: 147 us -> 140 us  [gather_block(): pl.pallas_call(functools.partial(gather_kernel, chips, leaves), out_shape...]
    concatenate x0 -> x2, other arithmetic: none -> 4.39 us  [finish_block(): jnp.concatenate([jnp.dot(whole_panel[:, s * step:], block, preferred_elem...]
    squeeze x2 -> x0, local copies, waits for them, and re-layouts: 4.03 us -> none  [finish_block(): panels[r]]
  transfers between devices with their start and end apart: 1 -> 1, of which waited for: 0 -> 0; matrix products, arithmetic and copies ran while one was open for 9% -> 8% of each run, Pallas kernels for 26% -> 25%
where the time goes in v4:
time: 286 us; the launch traced here: 283 us
  Pallas kernels  187 us (65%)
  matrix products  40.1 us (14%)
  between operations  37.5 us (13%)
  other arithmetic  10.6 us (4%)
  local copies, waits for them, and re-layouts  7.76 us (3%)
    pallas_call x2, Pallas kernels, gather_block(): pl.pallas_call(functools.partial(gather_kernel, chips, leaves), out_shape...  140 us
    pallas_call x1, Pallas kernels, line_sum(): pl.pallas_call(functools.partial(line_sum_kernel, chips), out_shape=jax.S...  46.7 us
    dot_general x8, matrix products, finish_block(): jnp.dot(whole_panel[:, s * step:], block, preferred_element_type=jnp.floa...  14.6 us
    dot_general x8, matrix products, finish_block(): lax.dot_general(block, linv[s * step:], (((0,), (0,)), ((), ())), preferr...  14.2 us
    dot_general x2, matrix products, finish_block(): lax.dot_general(upper, cross, (((0,), (0,)), ((), ())), precision=HIGH)  8.58 us
  transfers between devices with their start and end apart: 1, of which 0 were waited for; matrix products, arithmetic and copies ran while one was open for 8% of the time, Pallas kernels for 25%

profile of v4, /device:TPU:0, one launch (start us, length us, event | category | flops | bytes accessed | tf_op | source)
XLA Modules:
  0.0 283.2 jit_solution(318771095621999698)
XLA Ops:
  7.2 0.7 constant_dynamic-slice_fusion
  16.3 1.1 constant_dynamic-slice_fusion.4
  17.7 1.0 pad_maximum_fusion.2
  24.4 0.7 fusion.40
  35.5 0.6 broadcast_in_dim.45
  36.1 0.7 bitcast_multiply_fusion.1.panel_ref
  36.8 71.7 %gather_0.1 = (bf16[512,2048]{1,0:T(8,128)(2,1)}, bf16[2048,512]{1,0:T(8,128)(2,1)}, bf16[1536,512]{1,0:T(8,128)(2,1)}, bf16[1024,512]{1,0:T(8,128)(2,1)}, bf16[512,512]{1,0:T(8,128)(2,1)}) custom-call(bf16[512,256]{1,0:T(8,128)(2,1)} %bitcast_multiply_fusion.1.panel_ref, bf16[2048,256]{1,0:T(8,128)(2,1)} %bitcast.92), custom_call_target="tpu_custom_call" | custom-call | bytes 209715200 | tf_op jit(solution)/shard_map/gather_0/pallas_call | solution.py:193
  108.5 3.3 %fusion.37 = f32[512,256]{1,0:T(8,128)} fusion(bf16[2048,512]{1,0:T(8,128)(2,1)} %get-tuple-element.15, bf16[1,2048,256]{2,1,0:T(8,128)(2,1)S(1)} %copy-done), kind=kOutput, calls=%fused_computation.82 | convolution fusion | flops 536870912 | bytes 3670016 | tf_op jit(solution)/shard_map/dot_general | solution.py:359
  111.9 3.0 %fusion.42 = f32[512,512]{0,1:T(8,128)S(1)} fusion(bf16[512,2048]{1,0:T(8,128)(2,1)} %get-tuple-element.19, bf16[2048,512]{1,0:T(8,128)(2,1)S(1)} %copy-done.4), kind=kOutput, calls=%fused_computation.87 | convolution fusion | flops 1073741824 | bytes 5242880 | tf_op jit(solution)/shard_map/dot_general | solution.py:350
  114.9 1.4 fusion.11
  116.5 2.1 fusion.3
  118.6 1.3 fusion.17
  119.8 1.7 fusion.7
  122.1 1.1 fusion.29
  124.0 0.7 bitcast_multiply_fusion.panel_ref
  124.7 3.9 %pad_maximum_fusion = f32[512,2048]{0,1:T(8,128)} fusion(f32[512,512]{0,1:T(8,128)S(1)} %fusion.24, f32[512,512]{0,1:T(8,128)} %fusion.7, f32[512,512]{0,1:T(8,128)} %fusion.3, f32[512,512]{0,1:T(8,128)S(1)} %fusion.42), kind=kLoop, calls=%fused_computation | loop fusion | flops 3145728 | bytes 8388608 | tf_op jit(solution)/shard_map/concatenate | solution.py:348
  128.7 2.1 convolution_negate_fusion.1
  130.8 4.5 %convolution_subtract_fusion.1 = f32[2048,256]{1,0:T(8,128)S(1)} fusion(f32[512,256]{1,0:T(8,128)S(1)} %convolution_negate_fusion.1, f32[512,256]{1,0:T(8,128)} %fusion.29, f32[512,256]{1,0:T(8,128)} %fusion.17, f32[512,256]{1,0:T(8,128)} %fusion.11, f32[512,256]{1,0:T(8,128)} %fusion.37, f32[512,512]{0,1:T(8,128)S(1)} %fusion.24, ...), kind=kOutput, calls=%fused_computation.4 | convolution fusion | flops 1615855616 | bytes 8912896 | tf_op jit(solution)/shard_map/dot_general | solution.py:366
  135.8 0.9 copy-done.2
  136.7 1.6 broadcast_multiply_fusion.rest_0_
  138.2 68.7 %gather_1.1 = (bf16[512,2048]{1,0:T(8,128)(2,1)}, bf16[2048,512]{1,0:T(8,128)(2,1)}, bf16[1536,512]{1,0:T(8,128)(2,1)}, bf16[1024,512]{1,0:T(8,128)(2,1)}, bf16[...) custom-call(bf16[512,256]{1,0:T(8,128)(2,1)} %bitcast_multiply_fusion.panel_ref, bf16[2048,256]{1,0:T(8,128)(2,1)} %bitcast.93, ...), custom_call_target="tpu_custom_call" | custom-call | bytes 209715200 | tf_op jit(solution)/shard_map/gather_1/pallas_call | solution.py:193
  207.0 3.3 %fusion.35 = f32[512,256]{1,0:T(8,128)} fusion(bf16[2048,512]{1,0:T(8,128)(2,1)} %get-tuple-element.20, bf16[1,2048,256]{2,1,0:T(8,128)(2,1)S(1)} %copy-done.1), kind=kOutput, calls=%fused_computation.80 | convolution fusion | flops 536870912 | bytes 3670016 | tf_op jit(solution)/shard_map/dot_general | solution.py:359
  210.3 3.0 %fusion.43 = f32[512,512]{0,1:T(8,128)S(1)} fusion(bf16[512,2048]{1,0:T(8,128)(2,1)} %get-tuple-element.24, bf16[2048,512]{1,0:T(8,128)(2,1)S(1)} %copy-done.3), kind=kOutput, calls=%fused_computation.88 | convolution fusion | flops 1073741824 | bytes 5242880 | tf_op jit(solution)/shard_map/dot_general | solution.py:350
  213.3 1.4 fusion.9
  214.9 2.0 fusion.1
  216.9 1.3 fusion.15
  218.2 1.7 fusion.5
  220.4 1.1 fusion.27
  221.5 1.8 reduce_sum.9
  223.6 46.7 %line_sum.1 = f32[512,512]{1,0:T(8,128)S(1)} custom-call(f32[512,512]{1,0:T(8,128)S(1)} %pad_maximum_fusion.3.part_ref), custom_call_target="tpu_custom_call" | custom-call | tf_op jit(solution)/shard_map/line_sum/pallas_call | solution.py:313
  270.8 0.6 convolution_negate_fusion
  272.3 4.1 %fusion = f32[1,2048,256]{2,1,0:T(8,128)} fusion(f32[512,256]{1,0:T(8,128)S(1)} %convolution_negate_fusion, f32[512,256]{1,0:T(8,128)S(1)} %copy-done.14, f32[512,256]{1,0:T(8,128)S(1)} %copy-done.27, f32[512,256]{1,0:T(8,128)S(1)} %copy-done.28, f32[512,256]{1,0:T(8,128)S(1)} %copy-done.12, f32[512,512]{0,1:T(8,128)S(1)} %fusion.20, ...), kind=kOutput, calls=%fused_computation.3 | convolution fusion | flops 1615855616 | bytes 8912896 | tf_op jit(solution)/shard_map/dot_general | solution.py:366
  (94 shorter events, 5.5 us)
Async XLA Ops:
  7.2 121.5 %all-reduce.2.cloned.1.call-start = ((), (), s32[]{:S(2)}) async-start(), calls=%async_computation | async-start | bytes 2097152 | tf_op jit(solution)/shard_map/psum | solution.py:397
  17.5 1.2 copy-start.19
  17.5 17.8 %copy-start.24 = (s32[1,4,2]{1,2,0:T(2,128)S(1)}, s32[1,4,2]{1,2,0:T(2,128)}, u32[]{:S(2)}) copy-start(s32[1,4,2]{1,2,0:T(2,128)} %param.14) | copy-start | bytes 100
  17.6 18.4 %copy-start.15 = (bf16[1,512,256]{2,1,0:T(8,128)(2,1)S(1)}, bf16[1,512,256]{2,1,0:T(8,128)(2,1)}, u32[]{:S(2)}) copy-start(bf16[1,512,256]{2,1,0:T(8,128)(2,1)} %param.12) | copy-start | bytes 786436
  18.7 89.8 %copy-start = (bf16[1,2048,256]{2,1,0:T(8,128)(2,1)S(1)}, bf16[1,2048,256]{2,1,0:T(8,128)(2,1)}, u32[]{:S(2)}) copy-start(bf16[1,2048,256]{2,1,0:T(8,128)(2,1)} %param.11) | copy-start | bytes 3145732
  108.5 3.3 %copy-start.4 = (bf16[2048,512]{1,0:T(8,128)(2,1)S(1)}, bf16[2048,512]{1,0:T(8,128)(2,1)}, u32[]{:S(2)}) copy-start(bf16[2048,512]{1,0:T(8,128)(2,1)} %get-tuple-element.15) | copy-start | bytes 6291460
  111.9 3.0 %copy-start.21 = (bf16[1536,512]{1,0:T(8,128)(2,1)S(1)}, bf16[1536,512]{1,0:T(8,128)(2,1)}, u32[]{:S(2)}) copy-start(bf16[1536,512]{1,0:T(8,128)(2,1)} %get-tuple-element.16) | copy-start | bytes 4718596
  114.9 1.6 copy-start.18
  116.5 2.1 copy-start.23
  119.8 1.7 copy-start.6
  121.6 1.6 copy-start.25
  121.6 2.4 copy-start.16
  121.6 3.1 %copy-start.26 = (s32[4]{0:T(128)S(1)}, s32[4]{0:T(128)}, u32[]{:S(2)}) copy-start(s32[4]{0:T(128)} %param.19) | copy-start | bytes 52
  128.7 2.1 copy-start.7
  128.7 2.1 copy-start.8
  130.8 4.5 %copy-start.11 = (f32[512,256]{1,0:T(8,128)}, f32[512,256]{1,0:T(8,128)S(1)}, u32[]{:S(2)}) copy-start(f32[512,256]{1,0:T(8,128)S(1)} %convolution_negate_fusion.1) | copy-start | bytes 1572868
  135.3 1.3 copy-start.2
  138.2 68.8 %copy-start.1 = (bf16[1,2048,256]{2,1,0:T(8,128)(2,1)S(1)}, bf16[1,2048,256]{2,1,0:T(8,128)(2,1)}, u32[]{:S(2)}) copy-start(bf16[1,2048,256]{2,1,0:T(8,128)(2,1)} %param.15) | copy-start | bytes 3145732
  207.0 3.3 %copy-start.3 = (bf16[2048,512]{1,0:T(8,128)(2,1)S(1)}, bf16[2048,512]{1,0:T(8,128)(2,1)}, u32[]{:S(2)}) copy-start(bf16[2048,512]{1,0:T(8,128)(2,1)} %get-tuple-element.20) | copy-start | bytes 6291460
  210.2 3.0 %copy-start.20 = (bf16[1536,512]{1,0:T(8,128)(2,1)S(1)}, bf16[1536,512]{1,0:T(8,128)(2,1)}, u32[]{:S(2)}) copy-start(bf16[1536,512]{1,0:T(8,128)(2,1)} %get-tuple-element.21) | copy-start | bytes 4718596
  213.3 1.6 copy-start.17
  214.9 2.0 copy-start.22
  218.2 1.7 copy-start.5
  223.5 46.8 %copy-start.9 = (f32[512,512]{0,1:T(8,128)S(1)}, f32[512,512]{0,1:T(8,128)}, u32[]{:S(2)}) copy-start(f32[512,512]{0,1:T(8,128)} %fusion.1) | copy-start | bytes 3145732
  223.5 46.8 %copy-start.10 = (f32[512,512]{0,1:T(8,128)S(1)}, f32[512,512]{0,1:T(8,128)}, u32[]{:S(2)}) copy-start(f32[512,512]{0,1:T(8,128)} %fusion.5) | copy-start | bytes 3145732
  270.7 1.0 copy-start.12
  270.7 1.2 copy-start.14
  270.8 1.3 copy-start.27
  270.8 1.5 copy-start.28
  272.3 4.1 %copy-start.13 = (f32[512,256]{1,0:T(8,128)}, f32[512,256]{1,0:T(8,128)S(1)}, u32[]{:S(2)}) copy-start(f32[512,256]{1,0:T(8,128)S(1)} %convolution_negate_fusion) | copy-start | bytes 1572868
Sparse Core Ops, SparseCore 0:
  18.8 66.4 all-reduce.1
